TPU v7x, 32 devices: a whole 2x2x4 slice. The times are simulated.
32 devices in a mesh: rep: 8 (over y, x, core), grp: 4 (over z).
Axes of the slice: x: 2, y: 2, z: 4, core: 2. Of those that a mesh axis runs over, the one named last changes fastest.
Arguments:
- image_tokens: bfloat16 [8, 580, 384], P('rep', 'grp'), may hold values from -6 to 6
- valid_count: int32 [8], P('rep'), may hold values from 436 to 580
- first_gain: bfloat16 [384], P('grp'), may hold values from 0.5 to 1.5
- first_bias: bfloat16 [384], P('grp'), may hold values from -4 to 4
- heads_weight: bfloat16 [384, 1152], P('grp'), may hold values from -0.3125 to 0.3125
- heads_bias: bfloat16 [768], P('grp'), may hold values from -6 to 6
- mixing_weight: bfloat16 [384, 384], P('grp'), may hold values from -3.5 to 3.5
- mixing_bias: bfloat16 [384], P('grp'), may hold values from -4 to 4
- second_gain: bfloat16 [384], P('grp'), may hold values from 0.5 to 1.5
- second_bias: bfloat16 [384], P('grp'), may hold values from -4 to 4
- expand_weight: bfloat16 [384, 1536], P('grp'), may hold values from -0.3125 to 0.3125
- expand_bias: bfloat16 [1536], P('grp'), may hold values from -6 to 6
- reduce_weight: bfloat16 [1536, 384], P('grp'), may hold values from -0.21875 to 0.21875
- reduce_bias: bfloat16 [384], P('grp'), may hold values from -4 to 4
- output_cotangent: bfloat16 [8, 580, 384], P('rep', 'grp'), may hold values from -6 to 6
Outputs:
- block_output: bfloat16 [8, 580, 384], P('rep', 'grp')
- input_gradient: float32 [8, 580, 384], P('rep', 'grp')
- first_gain_gradient: float32 [384], P('grp')
- first_bias_gradient: float32 [384], P('grp')
- heads_weight_gradient: float32 [384, 1152], P('grp')
- heads_bias_gradient: float32 [768], P('grp')
- mixing_weight_gradient: float32 [384, 384], P('grp')
- mixing_bias_gradient: float32 [384], P('grp')
- second_gain_gradient: float32 [384], P('grp')
- second_bias_gradient: float32 [384], P('grp')
- expand_weight_gradient: float32 [384, 1536], P('grp')
- expand_bias_gradient: float32 [1536], P('grp')
- reduce_weight_gradient: float32 [1536, 384], P('grp')
- reduce_bias_gradient: float32 [384], P('grp')
Inputs may be any that keep to these rules, and one draw needn't show every extreme that they name: Image i's first valid_count[i] token slots hold real tokens, the rest are padding.
All inputs are finite; a program needn't handle non-finite values.
Results may differ from a plain program's by a relative error of at most 0.0091.
Values may be sent and summed in bfloat16 or wider, within the bound.
A program may use at most 64 MiB of HBM per device.

v0:
```python
import jax
import jax.numpy as jnp
from jax import lax
from jax.sharding import PartitionSpec as P

HEADS = 6
HEAD_DIM = 64


norm_eps = 1e-06
masked_score = -1000000000.0


def layer_norm(hidden, gain_vec, bias_vec):
    average = jnp.mean(hidden, axis=-1, keepdims=True)
    centered = hidden - average
    variance = jnp.mean(centered * centered, axis=-1, keepdims=True)
    return centered * lax.rsqrt(variance + norm_eps) * gain_vec + bias_vec


def column_sum(values_low):
    return jnp.sum(values_low.astype(jnp.float32), axis=0)


def on_device(
    image_tokens,
    valid_count,
    first_gain,
    first_bias,
    heads_weight,
    heads_bias,
    mixing_weight,
    mixing_bias,
    second_gain,
    second_bias,
    expand_weight,
    expand_bias,
    reduce_weight,
    reduce_bias,
    output_cotangent,
):
    gathered = (
        lax.all_gather(first_gain, "grp", axis=0, tiled=True),
        lax.all_gather(first_bias, "grp", axis=0, tiled=True),
        lax.all_gather(heads_weight, "grp", axis=0, tiled=True),
        lax.all_gather(heads_bias, "grp", axis=0, tiled=True),
        lax.all_gather(mixing_weight, "grp", axis=0, tiled=True),
        lax.all_gather(mixing_bias, "grp", axis=0, tiled=True),
        lax.all_gather(second_gain, "grp", axis=0, tiled=True),
        lax.all_gather(second_bias, "grp", axis=0, tiled=True),
        lax.all_gather(expand_weight, "grp", axis=0, tiled=True),
        lax.all_gather(expand_bias, "grp", axis=0, tiled=True),
        lax.all_gather(reduce_weight, "grp", axis=0, tiled=True),
        lax.all_gather(reduce_bias, "grp", axis=0, tiled=True),
    )
    (
        gain_one,
        bias_one,
        w_heads,
        b_heads,
        w_mixing,
        b_mixing,
        gain_two,
        bias_two,
        w_expand,
        b_expand,
        w_reduce,
        b_reduce,
    ) = gathered
    image_count, span_rows, model_width = image_tokens.shape
    row_count = image_count * span_rows
    padded_len = span_rows * lax.axis_size("grp")
    score_scale = HEAD_DIM ** (-0.5)
    f32 = jnp.float32
    bf16 = jnp.bfloat16
    tokens_f = image_tokens.astype(f32).reshape(row_count, model_width)
    normed_one, norm_one_pull = jax.vjp(
        layer_norm, tokens_f, gain_one.astype(f32), bias_one.astype(f32)
    )
    normed_low = normed_one.astype(bf16)
    projected = jnp.dot(normed_low, w_heads, preferred_element_type=f32)
    heads_bias_f = b_heads.astype(f32)
    query = (projected[:, :model_width] + heads_bias_f[:model_width]).astype(bf16)
    keys_local = projected[:, model_width : 2 * model_width].astype(bf16)
    values_local = (projected[:, 2 * model_width :] + heads_bias_f[model_width:]).astype(bf16)
    pair_local = jnp.concatenate([keys_local, values_local], 1).reshape(
        image_count, span_rows, 2 * model_width
    )
    pair_all = lax.all_gather(pair_local, "grp", axis=1, tiled=True)
    keys_h = pair_all[:, :, :model_width].reshape(image_count, padded_len, HEADS, HEAD_DIM)
    values_h = pair_all[:, :, model_width:].reshape(image_count, padded_len, HEADS, HEAD_DIM)
    query_h = query.reshape(image_count, span_rows, HEADS, HEAD_DIM)
    present = lax.broadcasted_iota(jnp.int32, (image_count, padded_len), 1) < valid_count[:, None]
    present = present[:, None, None, :]

    def scores_of():
        raw_scores = (
            jnp.einsum("iqhd,ikhd->ihqk", query_h, keys_h, preferred_element_type=f32) * score_scale
        )
        return jnp.where(present, raw_scores, masked_score)

    scores = scores_of()
    row_max = jnp.max(scores, axis=-1, keepdims=True)
    exp_scores = jnp.exp(scores - row_max)
    row_total = jnp.sum(exp_scores, axis=-1, keepdims=True)
    log_total = row_max + jnp.log(row_total)
    attn_prob = exp_scores / row_total
    mixed = jnp.einsum(
        "ihqk,ikhd->iqhd", attn_prob.astype(bf16), values_h, preferred_element_type=f32
    ).reshape(row_count, model_width)
    mixed_low = mixed.astype(bf16)
    after_attn = (
        tokens_f + jnp.dot(mixed_low, w_mixing, preferred_element_type=f32) + b_mixing.astype(f32)
    )
    normed_two, norm_two_pull = jax.vjp(
        layer_norm, after_attn, gain_two.astype(f32), bias_two.astype(f32)
    )
    normed_two_low = normed_two.astype(bf16)
    hidden_pre = jnp.dot(normed_two_low, w_expand, preferred_element_type=f32) + b_expand.astype(
        f32
    )
    activated, gelu_pull = jax.vjp(jax.nn.gelu, hidden_pre)
    activated_low = activated.astype(bf16)
    block_out = (
        after_attn
        + jnp.dot(activated_low, w_reduce, preferred_element_type=f32)
        + b_reduce.astype(f32)
    )
    gathered_back = (
        lax.all_gather(first_gain, "grp", axis=0, tiled=True),
        lax.all_gather(first_bias, "grp", axis=0, tiled=True),
        lax.all_gather(heads_weight, "grp", axis=0, tiled=True),
        lax.all_gather(heads_bias, "grp", axis=0, tiled=True),
        lax.all_gather(mixing_weight, "grp", axis=0, tiled=True),
        lax.all_gather(mixing_bias, "grp", axis=0, tiled=True),
        lax.all_gather(second_gain, "grp", axis=0, tiled=True),
        lax.all_gather(second_bias, "grp", axis=0, tiled=True),
        lax.all_gather(expand_weight, "grp", axis=0, tiled=True),
        lax.all_gather(expand_bias, "grp", axis=0, tiled=True),
        lax.all_gather(reduce_weight, "grp", axis=0, tiled=True),
        lax.all_gather(reduce_bias, "grp", axis=0, tiled=True),
    )
    back_heads = gathered_back[2]
    back_mixing = gathered_back[4]
    back_expand = gathered_back[8]
    back_reduce = gathered_back[10]
    out_cot = output_cotangent.astype(f32).reshape(row_count, model_width)
    reduce_cot = output_cotangent.reshape(row_count, model_width)
    grad_reduce_bias = column_sum(reduce_cot)
    grad_reduce_weight = jnp.dot(activated_low.T, reduce_cot, preferred_element_type=f32)
    grad_activated = jnp.dot(reduce_cot, back_reduce.T, preferred_element_type=f32)
    (grad_pre,) = gelu_pull(grad_activated)
    pre_cot = grad_pre.astype(bf16)
    grad_expand_bias = column_sum(pre_cot)
    grad_expand_weight = jnp.dot(normed_two_low.T, pre_cot, preferred_element_type=f32)
    grad_normed_two = jnp.dot(pre_cot, back_expand.T, preferred_element_type=f32)
    grad_after_norm, grad_gain_two, grad_bias_two = norm_two_pull(grad_normed_two)
    grad_after = out_cot + grad_after_norm
    attn_cot = grad_after.astype(bf16)
    grad_mixing_bias = column_sum(attn_cot)
    grad_mixing_weight = jnp.dot(mixed_low.T, attn_cot, preferred_element_type=f32)
    mixed_cot = jnp.dot(attn_cot, back_mixing.T, preferred_element_type=f32).astype(bf16)
    mixed_cot = mixed_cot.reshape(image_count, span_rows, HEADS, HEAD_DIM)
    prob_again = jnp.exp(scores_of() - log_total)
    grad_prob = jnp.einsum("iqhd,ikhd->ihqk", mixed_cot, values_h, preferred_element_type=f32)
    grad_values = jnp.einsum(
        "ihqk,iqhd->ikhd", prob_again.astype(bf16), mixed_cot, preferred_element_type=f32
    )
    inner_sum = jnp.sum(prob_again * grad_prob, axis=-1, keepdims=True)
    score_cot = (prob_again * (grad_prob - inner_sum)).astype(bf16)
    grad_query = (
        jnp.einsum("ihqk,ikhd->iqhd", score_cot, keys_h, preferred_element_type=f32) * score_scale
    )
    grad_keys = (
        jnp.einsum("ihqk,iqhd->ikhd", score_cot, query_h, preferred_element_type=f32) * score_scale
    )
    pair_grad = jnp.concatenate(
        [
            grad_keys.reshape(image_count, padded_len, model_width),
            grad_values.reshape(image_count, padded_len, model_width),
        ],
        2,
    )
    pair_owned = lax.psum_scatter(pair_grad, "grp", scatter_dimension=1, tiled=True)
    query_cot = grad_query.reshape(row_count, model_width).astype(bf16)
    pair_cot = pair_owned.reshape(row_count, 2 * model_width).astype(bf16)
    heads_cot = jnp.concatenate([query_cot, pair_cot], 1)
    grad_heads_bias = jnp.concatenate(
        [column_sum(query_cot), column_sum(pair_cot[:, model_width:])]
    )
    grad_heads_weight = jnp.dot(normed_low.T, heads_cot, preferred_element_type=f32)
    grad_normed_one = jnp.dot(heads_cot, back_heads.T, preferred_element_type=f32)
    grad_tokens_norm, grad_gain_one, grad_bias_one = norm_one_pull(grad_normed_one)
    input_gradient = (grad_after + grad_tokens_norm).reshape(image_count, span_rows, model_width)
    group_part = (
        lax.psum_scatter(grad_gain_one, "grp", scatter_dimension=0, tiled=True),
        lax.psum_scatter(grad_bias_one, "grp", scatter_dimension=0, tiled=True),
        lax.psum_scatter(grad_heads_weight, "grp", scatter_dimension=0, tiled=True),
        lax.psum_scatter(grad_heads_bias, "grp", scatter_dimension=0, tiled=True),
        lax.psum_scatter(grad_mixing_weight, "grp", scatter_dimension=0, tiled=True),
        lax.psum_scatter(grad_mixing_bias, "grp", scatter_dimension=0, tiled=True),
        lax.psum_scatter(grad_gain_two, "grp", scatter_dimension=0, tiled=True),
        lax.psum_scatter(grad_bias_two, "grp", scatter_dimension=0, tiled=True),
        lax.psum_scatter(grad_expand_weight, "grp", scatter_dimension=0, tiled=True),
        lax.psum_scatter(grad_expand_bias, "grp", scatter_dimension=0, tiled=True),
        lax.psum_scatter(grad_reduce_weight, "grp", scatter_dimension=0, tiled=True),
        lax.psum_scatter(grad_reduce_bias, "grp", scatter_dimension=0, tiled=True),
    )
    totals = lax.psum(
        (
            group_part[0],
            group_part[1],
            group_part[2],
            group_part[3],
            group_part[4],
            group_part[5],
            group_part[6],
            group_part[7],
            group_part[8],
            group_part[9],
            group_part[10],
            group_part[11],
        ),
        "rep",
    )
    block_output = block_out.reshape(image_count, span_rows, model_width).astype(bf16)
    return (
        block_output,
        input_gradient,
        totals[0],
        totals[1],
        totals[2],
        totals[3],
        totals[4],
        totals[5],
        totals[6],
        totals[7],
        totals[8],
        totals[9],
        totals[10],
        totals[11],
    )


def solution(mesh):
    return jax.shard_map(
        on_device,
        mesh=mesh,
        in_specs=(
            P("rep", "grp", None),
            P("rep"),
            P("grp"),
            P("grp"),
            P("grp", None),
            P("grp"),
            P("grp", None),
            P("grp"),
            P("grp"),
            P("grp"),
            P("grp", None),
            P("grp"),
            P("grp", None),
            P("grp"),
            P("rep", "grp", None),
        ),
        out_specs=(
            P("rep", "grp", None),
            P("rep", "grp", None),
            P("grp"),
            P("grp"),
            P("grp", None),
            P("grp"),
            P("grp", None),
            P("grp"),
            P("grp"),
            P("grp"),
            P("grp", None),
            P("grp"),
            P("grp", None),
            P("grp"),
        ),
        check_vma=False,
    )
```

profile of v0, /device:TPU:0, one launch (start us, length us, event | category | flops | bytes accessed | tf_op | source)
XLA Modules:
  0.0 835.5 jit_solution(8412797288207529996)
XLA Ops:
  9.4 1.3 fusion.55
  13.0 1.1 fusion.27
  20.8 14.6 %all-reduce.19 = (bf16[768]{0:T(1024)(128)(2,1)S(1)}, bf16[384]{0:T(512)(128)(2,1)S(1)}, bf16[384]{0:T(512)(128)(2,1)S(1)}, bf16[384]{0:T(512)(128)(2,1)S(1)}, b...) all-reduce(bf16[768]{0:T(1024)(128)(2,1)S(1)} %dynamic-update-slice, ...), channel_id=1, replica_groups=mesh['rep'=8,'grp'=4] {'grp'}, use_global_device_ids=true, to_apply=%add.2 | all-reduce | flops 3072 | bytes 12288
  35.4 11.9 %all-gather.2 = bf16[4,1,384]{2,1,0:T(2,128)(2,1)S(1)} all-gather(bf16[1,1,384]{2,1,0:T(2,128)(2,1)S(1)} %reshape.266), channel_id=1, replica_groups=mesh['rep'=8,'grp'=4] {'grp'}, dimensions={0}, use_global_device_ids=true | all-gather | bytes 3840 | tf_op jit(solution)/shard_map/all_gather | solution.py:52
  47.3 25.8 %all_gather.45 = bf16[384,1152]{1,0:T(8,128)(2,1)S(1)} all-gather(bf16[96,1152]{1,0:T(8,128)(2,1)} %param.19), channel_id=1, replica_groups=mesh['rep'=8,'grp'=4] {'grp'}, dimensions={0}, use_global_device_ids=true | all-gather | bytes 1105920 | tf_op jit(solution)/shard_map/all_gather | solution.py:45
  74.1 1.3 fusion.46
  75.7 22.6 %all-gather.1 = bf16[4,145,768]{2,1,0:T(8,128)(2,1)S(1)} all-gather(bf16[1,145,768]{2,1,0:T(8,128)(2,1)S(1)} %maximum_bitcast_fusion), channel_id=2, replica_groups=mesh['rep'=8,'grp'=4] {'grp'}, dimensions={0}, use_global_device_ids=true | all-gather | bytes 1113600 | tf_op jit(solution)/shard_map/all_gather | solution.py:89
  101.2 14.2 %all_gather.48 = bf16[384,384]{1,0:T(8,128)(2,1)S(1)} all-gather(bf16[96,384]{1,0:T(8,128)(2,1)S(1)} %copy-done.27), channel_id=1, replica_groups=mesh['rep'=8,'grp'=4] {'grp'}, dimensions={0}, use_global_device_ids=true | all-gather | bytes 368640 | tf_op jit(solution)/shard_map/all_gather | solution.py:47
  115.4 1.3 copy.49
  119.2 1.7 convolution_add_fusion
  121.0 3.3 convert_reduce_fusion
  124.3 1.1 multiply_reduce_fusion.1
  128.6 3.1 multiply_reduce_fusion
  132.0 1.9 copy.54
  133.9 2.2 multiply_convert_fusion
  136.5 1.9 copy.53
  138.4 3.0 pad_maximum_fusion
  141.4 477.6 %all-reduce.24 = bf16[1,580,768]{2,0,1:T(2,128)(2,1)} all-reduce(f32[1,580,768]{2,0,1:T(1,128)S(1)} %pad_maximum_fusion), channel_id=3, replica_groups=mesh['rep'=8,'grp'=4] {'grp'}, use_global_device_ids=true, to_apply=%region_9.10.clone | all-reduce | flops 445440 | bytes 2672640
  618.9 1.5 constant_dynamic-slice_fusion
  621.3 1.8 fusion.32
  623.3 2.1 fusion.35
  625.5 2.0 fusion.49
  630.2 29.0 %reduce-scatter.5.cloned.1.call-done = f32[96,1152]{1,0:T(8,128)} async-done(((f32[384,1152]{1,0:T(8,128)}), f32[96,1152]{1,0:T(8,128)}) %reduce-scatter.5.cloned.1.call-update) | async-done | bytes 442384 | tf_op jit(solution)/shard_map/reduce_scatter | solution.py:198
  659.2 49.5 %reduce-scatter.11.cloned.1.call-done = f32[384,384]{1,0:T(8,128)} async-done(((f32[1536,384]{1,0:T(8,128)}), f32[384,384]{1,0:T(8,128)}) %reduce-scatter.11.cloned.1.call-update) | async-done | bytes 589840 | tf_op jit(solution)/shard_map/reduce_scatter | solution.py:206
  708.7 49.8 %reduce-scatter.9.cloned.1.call-done = f32[96,1536]{1,0:T(8,128)} async-done(((f32[384,1536]{1,0:T(8,128)}), f32[96,1536]{1,0:T(8,128)}) %reduce-scatter.9.cloned.1.call-update) | async-done | bytes 589840 | tf_op jit(solution)/shard_map/reduce_scatter | solution.py:204
  759.2 17.2 %all-reduce.18 = (f32[384]{0:T(512)S(1)}, f32[384]{0:T(512)S(1)}, f32[768]{0:T(1024)S(1)}, f32[384]{0:T(512)S(1)}, f32[384]{0:T(512)S(1)}, /*index=5*/f32[384]{0:T(512)S(1)}, f32[1536]{0:T(1024)S(1)}, f32[384]{0:T(512)S(1)}) all-reduce(f32[384]{0:T(512)S(1)} %get-tuple-element.72, ...), channel_id=4, replica_groups=mesh['rep'=8,'grp'=4] {'grp'}, use_global_device_ids=true, to_apply=%region_13.14.clone | all-reduce | flops 4608 | bytes 36864
  777.9 12.8 %all-reduce.16 = (f32[96]{0:T(128)}, f32[96]{0:T(128)}, f32[192]{0:T(256)}, f32[96]{0:T(128)}, f32[96]{0:T(128)}, /*index=5*/f32[96]{0:T(128)}, f32[384]{0:T(512)}, f32[96]{0:T(128)}) all-reduce(f32[96]{0:T(128)S(1)} %dynamic-slice.10, f32[96]{0:T(128)S(1)} %dynamic-slice.12, ...), channel_id=1, replica_groups=mesh['rep'=8,'grp'=4] {'rep'}, use_global_device_ids=true, to_apply=%region_14.15 | all-reduce | flops 1152 | bytes 9216 | tf_op jit(solution)/shard_map/psum | solution.py:209
  790.7 2.4 fusion.9
  793.1 29.4 %all-reduce.23.cloned.1.call-done = (f32[96,1152]{1,0:T(8,128)}, f32[96,384]{1,0:T(8,128)}, f32[96,1536]{1,0:T(8,128)}, f32[384,384]{1,0:T(8,128)}) async-done(((f32[96,1152]{1,0:T(8,128)}, f32[96,384]{1,0:T(8,128)}, f32[96,1536]{1,0:T(8,128)}, f32[384,384]{1,0:T(8,128)}), (f32[96,1152]{1,0:T(8,128)}, f32[96,384]{1,0:T(8,128)}, f32[96,1536]{1,0:T(8,128)}, ...) | async-done | bytes 1769488 | tf_op jit(solution)/shard_map/psum | solution.py:209
  822.5 1.9 copy.76
  824.3 1.6 copy.77
  825.9 1.9 copy.78
  (172 shorter events, 23.4 us)
Async XLA Ops:
  7.2 112.0 %all-gather.6.cloned.1.call-start = ((), (), s32[]{:S(2)}) async-start(), calls=%async_computation.4 | async-start | bytes 1474560 | tf_op jit(solution)/shard_map/all_gather | solution.py:51
  7.9 113.1 %all-gather.8.cloned.1.call-start = ((), (), s32[]{:S(2)}) async-start(), calls=%async_computation.5 | async-start | bytes 1474560 | tf_op jit(solution)/shard_map/all_gather | solution.py:53
  8.7 621.6 %reduce-scatter.7.cloned.1.call-start = ((), (), s32[]{:S(2)}) async-start(), calls=%async_computation.7 | async-start | bytes 737280 | tf_op jit(solution)/shard_map/reduce_scatter | solution.py:200
  14.1 21.3 %copy-start.32 = (f32[145]{0:T(256)}, f32[145]{0:T(256)S(1)}, u32[]{:S(2)}) copy-start(f32[145]{0:T(256)S(1)} %fusion.27) | copy-start | bytes 1744
  35.4 40.1 %copy-start.28 = (f32[384]{0:T(512)}, f32[384]{0:T(512)S(1)}, u32[]{:S(2)}) copy-start(f32[384]{0:T(512)S(1)} %convert_element_type.122) | copy-start | bytes 4612
  75.7 24.0 %copy-start.18 = (bf16[145,384]{0,1:T(8,128)(2,1)}, bf16[145,384]{0,1:T(8,128)(2,1)S(1)}, u32[]{:S(2)}) copy-start(bf16[145,384]{0,1:T(8,128)(2,1)S(1)} %copy.50) | copy-start | bytes 334084
  115.4 2.9 copy-start.11
  115.4 3.8 copy-start.30
  119.0 6.5 copy-start
  121.0 3.3 copy-start.7
  121.0 3.3 copy-start.4
  124.3 2.4 copy-start.16
  124.3 2.5 copy-start.25
  131.8 527.5 %reduce-scatter.5.cloned.1.call-start = ((), (), s32[]{:S(2)}) async-start(), calls=%async_computation.6 | async-start | bytes 2211840 | tf_op jit(solution)/shard_map/reduce_scatter | solution.py:198
  141.3 479.1 %copy-start.6 = (bf16[1,580,384]{1,2,0:T(8,128)(2,1)S(1)}, bf16[1,580,384]{1,2,0:T(8,128)(2,1)}, u32[]{:S(2)}) copy-start(bf16[1,580,384]{1,2,0:T(8,128)(2,1)} %copy-done.5) | copy-start | bytes 1336324
  618.9 2.4 copy-start.3
  618.9 2.4 copy-start.29
  620.5 2.6 copy-start.20
  623.2 85.5 %reduce-scatter.11.cloned.1.call-start = ((), (), s32[]{:S(2)}) async-start(), calls=%async_computation.9 | async-start | bytes 2949120 | tf_op jit(solution)/shard_map/reduce_scatter | solution.py:206
  625.4 4.2 copy-start.40
  625.4 4.2 copy-start.10
  625.4 4.2 copy-start.21
  625.4 133.1 %reduce-scatter.9.cloned.1.call-start = ((), (), s32[]{:S(2)}) async-start(), calls=%async_computation.8 | async-start | bytes 2949120 | tf_op jit(solution)/shard_map/reduce_scatter | solution.py:204
  627.5 2.7 copy-start.33
  627.5 131.4 %copy-start.14 = (f32[145,384]{1,0:T(8,128)S(1)}, f32[145,384]{1,0:T(8,128)}, u32[]{:S(2)}) copy-start(f32[145,384]{1,0:T(8,128)} %copy-done.13) | copy-start | bytes 668164
  627.5 131.4 %copy-start.35 = (f32[145]{0:T(256)S(1)}, f32[145]{0:T(256)}, u32[]{:S(2)}) copy-start(f32[145]{0:T(256)} %copy-done.34) | copy-start | bytes 1744
  627.5 195.0 %all-reduce.23.cloned.1.call-start = ((), (), s32[]{:S(2)}) async-start(), calls=%async_computation.10 | async-start | bytes 3538944 | tf_op jit(solution)/shard_map/psum | solution.py:209
  629.6 129.6 %copy-start.36 = (f32[384]{0:T(512)S(1)}, f32[384]{0:T(512)}, u32[]{:S(2)}) copy-start(f32[384]{0:T(512)} %get-tuple-element.104) | copy-start | bytes 4612
  629.6 129.6 %copy-start.37 = (f32[1536]{0:T(1024)S(1)}, f32[1536]{0:T(1024)}, u32[]{:S(2)}) copy-start(f32[1536]{0:T(1024)} %get-tuple-element.128) | copy-start | bytes 18436
  629.6 129.6 %copy-start.38 = (f32[384]{0:T(512)S(1)}, f32[384]{0:T(512)}, u32[]{:S(2)}) copy-start(f32[384]{0:T(512)} %get-tuple-element.70) | copy-start | bytes 4612
  629.6 129.5 %copy-start.39 = (f32[384]{0:T(512)S(1)}, f32[384]{0:T(512)}, u32[]{:S(2)}) copy-start(f32[384]{0:T(512)} %get-tuple-element.74) | copy-start | bytes 4612
  822.5 5.4 copy-start.26
  (16 other events, 27.2 us)
Sparse Core Ops, SparseCore 0:
  9.6 33.8 all-gather.5
  45.0 43.0 all-gather.7
  131.9 26.1 reduce-scatter.6
  623.3 35.9 reduce-scatter.4
  661.5 47.1 reduce-scatter.10
  710.9 47.5 reduce-scatter.8
  762.5 59.8 all-reduce.22
where the time goes:
time: 836 us
  blocking collectives  597 us (71%)
  waiting for transfers between devices  159 us (19%)
  local copies, waits for them, and re-layouts  25.5 us (3%)
  matrix products  24.4 us (3%)
  between operations  19.5 us (2%)
  other arithmetic  9.87 us (1%)
    unnamed x3, blocking collectives  509 us
    reduce_scatter x1, waiting for transfers between devices, on_device(): lax.psum_scatter(grad_expand_weight, 'grp', scatter_dimension=0, tiled=True)  49.8 us
    reduce_scatter x1, waiting for transfers between devices, on_device(): lax.psum_scatter(grad_reduce_weight, 'grp', scatter_dimension=0, tiled=True)  49.5 us
    psum x1, waiting for transfers between devices, on_device(): lax.psum((group_part[0], group_part[1], group_part[2], group_part[3], gro...  29.4 us
    reduce_scatter x1, waiting for transfers between devices, on_device(): lax.psum_scatter(grad_heads_weight, 'grp', scatter_dimension=0, tiled=True)  29 us
    all_gather x1, blocking collectives, on_device(): lax.all_gather(heads_weight, 'grp', axis=0, tiled=True)  25.8 us
    all_gather x1, blocking collectives, on_device(): pair_all = lax.all_gather(pair_local, 'grp', axis=1, tiled=True)  22.6 us
    unnamed x112, local copies, waits for them, and re-layouts  18.5 us
  transfers between devices with their start and end apart: 7, of which 4 were waited for; matrix products, arithmetic and copies ran while one was open for 5% of the time, Pallas kernels for 0%

commit v1 on v0

v1 whole, which is shorter than its diff:
```python
import functools

import jax
import jax.numpy as jnp
from jax import lax
from jax.experimental import pallas as pl
from jax.experimental.pallas import tpu as pltpu
from jax.sharding import PartitionSpec as P

HEADS = 6
HEAD_DIM = 64
ROWS = 16
TEAM = 8

norm_eps = 1e-06
masked_score = -1000000000.0
f32 = jnp.float32
bf16 = jnp.bfloat16
MESH = pl.DeviceIdType.MESH
VMEM = pltpu.VMEM
LIMIT = 56 * 1024 * 1024


def up(count, unit):
    return (count + unit - 1) // unit * unit


def dot_nn(a, b):
    return lax.dot_general(a, b, (((1,), (0,)), ((), ())), preferred_element_type=f32)


def dot_nt(a, b):
    return lax.dot_general(a, b, (((1,), (1,)), ((), ())), preferred_element_type=f32)


def dot_tn(a, b):
    return lax.dot_general(a, b, (((0,), (0,)), ((), ())), preferred_element_type=f32)


def places():
    rep = lax.axis_index("rep")
    z = lax.axis_index("grp")
    core = lax.rem(rep, 2)
    spot = lax.rem(rep // 2, 4)
    base = rep - lax.rem(rep, TEAM)
    return rep, z, core, spot, base


def greet(devices):
    barrier = pltpu.get_barrier_semaphore()
    for device in devices:
        pl.semaphore_signal(barrier, inc=1, device_id=device, device_id_type=MESH)
    pl.semaphore_wait(barrier, len(devices))


def remote(src, dst, send, recv, device):
    copy = pltpu.make_async_remote_copy(
        src_ref=src, dst_ref=dst, send_sem=send, recv_sem=recv,
        device_id=device, device_id_type=MESH,
    )
    return copy


def team_devices():
    rep, z, core, spot, base = places()
    over_z = [(rep, lax.rem(z + d, 4)) for d in (1, 2, 3)]
    plane = [(base + lax.rem(spot + e, 4) * 2 + core, z) for e in (1, 2, 3)]
    twin = (base + spot * 2 + 1 - core, z)
    return over_z, plane, twin


def gather_kernel(
    w_ref, x_ref, s_ref, w_all, x_all, s_all,
    zs, zr, xs, xr, ss, sr, ps, pr, cs, cr, loc,
):
    rep, z, core, spot, base = places()
    over_z, plane, twin = team_devices()
    half = w_ref.shape[0] // 2
    cols = w_ref.shape[1] // 4
    rows = pl.ds(pl.multiple_of(core * half, 16), half)
    part = pl.ds(pl.multiple_of(spot * cols, 128), cols)
    greet(over_z + plane + [twin])
    copies = []
    for d in (1, 2, 3):
        copy = remote(w_ref.at[rows, part], w_all.at[z, rows, part], zs.at[d], zr.at[d], over_z[d - 1])
        copy.start()
        copies.append(copy)
    others = []
    for d in (1, 2, 3):
        a = remote(x_ref, x_all.at[z], xs.at[d], xr.at[d], over_z[d - 1])
        b = remote(s_ref, s_all.at[z], ss.at[d], sr.at[d], over_z[d - 1])
        a.start()
        b.start()
        others += [a, b]
    locals_ = []
    for k, (src, dst) in enumerate(((w_ref, w_all), (x_ref, x_all), (s_ref, s_all))):
        copy = pltpu.make_async_copy(src, dst.at[z], loc.at[k])
        copy.start()
        locals_.append(copy)
    spread = {}
    for d in (1, 2, 3):
        copies[d - 1].wait_recv()
        owner = lax.rem(z + 4 - d, 4)
        for e in (1, 2, 3):
            here = w_all.at[owner, rows, part]
            copy = remote(here, here, ps.at[d * 3 + e - 4], pr.at[d * 3 + e - 4], plane[e - 1])
            copy.start()
            spread[d, e] = copy
    crossed = []
    for d in (1, 2, 3):
        owner = lax.rem(z + 4 - d, 4)
        for e in (1, 2, 3):
            spread[d, e].wait_recv()
        here = w_all.at[owner, rows]
        copy = remote(here, here, cs.at[d], cr.at[d], twin)
        copy.start()
        crossed.append(copy)
    for copy in locals_:
        copy.wait()
    for copy in others:
        copy.wait()
    for copy in copies:
        copy.wait_send()
    for copy in spread.values():
        copy.wait_send()
    for copy in crossed:
        copy.wait()


def gather_call(w, x, s):
    dma = pltpu.SemaphoreType.DMA
    return pl.pallas_call(
        gather_kernel,
        out_shape=[jax.ShapeDtypeStruct((4,) + a.shape, a.dtype) for a in (w, x, s)],
        in_specs=[pl.BlockSpec(memory_space=VMEM)] * 3,
        out_specs=[pl.BlockSpec(memory_space=VMEM)] * 3,
        scratch_shapes=[dma((4,))] * 6 + [dma((9,))] * 2 + [dma((4,))] * 2 + [dma((3,))],
        compiler_params=pltpu.CompilerParams(
            collective_id=0, has_side_effects=True, vmem_limit_bytes=LIMIT
        ),
        name="gather",
    )(w, x, s)


def cot_kernel(m_ref, t_ref, m_all, t_all, ms, mr, ts, tr, loc):
    rep, z, core, spot, base = places()
    over_z, _, _ = team_devices()
    greet(over_z)
    sent = []
    for d in (1, 2, 3):
        a = remote(m_ref, m_all.at[z], ms.at[d], mr.at[d], over_z[d - 1])
        b = remote(t_ref, t_all.at[z], ts.at[d], tr.at[d], over_z[d - 1])
        a.start()
        b.start()
        sent += [a, b]
    c = pltpu.make_async_copy(m_ref, m_all.at[z], loc.at[0])
    e = pltpu.make_async_copy(t_ref, t_all.at[z], loc.at[1])
    c.start()
    e.start()
    c.wait()
    e.wait()
    for copy in sent:
        copy.wait()


def cot_call(m, t):
    dma = pltpu.SemaphoreType.DMA
    return pl.pallas_call(
        cot_kernel,
        out_shape=[jax.ShapeDtypeStruct((4,) + a.shape, a.dtype) for a in (m, t)],
        in_specs=[pl.BlockSpec(memory_space=VMEM)] * 2,
        out_specs=[pl.BlockSpec(memory_space=VMEM)] * 2,
        scratch_shapes=[dma((4,))] * 4 + [dma((2,))],
        compiler_params=pltpu.CompilerParams(
            collective_id=1, has_side_effects=True, vmem_limit_bytes=LIMIT
        ),
        name="cotangents",
    )(m, t)


def sum_kernel(
    g_ref, v_ref, o_ref, ov_ref,
    got1, h, got2, mine, got3, fin, v1, va, v2, vb, v3,
    s1, r1, s2, r2, s3, r3, s4, r4, s5, r5, sv, rv,
):
    rep, z, core, spot, base = places()
    over_z, plane, twin = team_devices()
    half = g_ref.shape[1] // 2
    cols = g_ref.shape[2] // 4
    rows = pl.ds(pl.multiple_of(core * half, 16), half)
    away = pl.ds(pl.multiple_of((1 - core) * half, 16), half)

    def part(index):
        return pl.ds(pl.multiple_of(index * cols, 128), cols)

    greet(over_z + plane + [twin])
    order = (2, 1, 3, 0)
    first = {}
    for d in order:
        to = lax.rem(z + d, 4)
        copy = remote(g_ref.at[to, away], got1.at[d], s1.at[d], r1.at[d], twin)
        copy.start()
        first[d] = copy
    vec = [remote(v_ref, v1, sv.at[0], rv.at[0], twin)]
    vec[0].start()
    second = {}
    for d in order:
        to = lax.rem(z + d, 4)
        first[d].wait_recv()
        h[d] = (g_ref[to, rows, :].astype(f32) + got1[d].astype(f32)).astype(bf16)
        for e in (1, 2, 3):
            there = lax.rem(spot + e, 4)
            copy = remote(h.at[d, :, part(there)], got2.at[d, e - 1],
                          s2.at[d * 3 + e - 1], r2.at[d * 3 + e - 1], plane[e - 1])
            copy.start()
            second[d, e] = copy
    vec[0].wait_recv()
    va[...] = v_ref[...] + v1[...]
    for e in (1, 2, 3):
        copy = remote(va, v2.at[e - 1], sv.at[e], rv.at[e], plane[e - 1])
        copy.start()
        vec.append(copy)
    third = {}
    for d in order:
        total = h[d, :, part(spot)].astype(f32)
        for e in (1, 2, 3):
            second[d, e].wait_recv()
            total += got2[d, e - 1].astype(f32)
        mine[d] = total.astype(bf16)
        if d:
            copy = remote(mine.at[d], got3.at[d], s3.at[d], r3.at[d], over_z[d - 1])
            copy.start()
            third[d] = copy
    for e in (1, 2, 3):
        vec[e].wait_recv()
    vb[...] = va[...] + v2[0] + v2[1] + v2[2]
    for d in (1, 2, 3):
        copy = remote(vb, v3.at[d - 1], sv.at[d + 3], rv.at[d + 3], over_z[d - 1])
        copy.start()
        vec.append(copy)
    total = mine[0].astype(f32)
    for d in (1, 2, 3):
        third[d].wait_recv()
        total += got3[d].astype(f32)
    fin[rows, part(spot)] = total.astype(bf16)
    fourth = []
    for e in (1, 2, 3):
        here = fin.at[rows, part(spot)]
        copy = remote(here, here, s4.at[e], r4.at[e], plane[e - 1])
        copy.start()
        fourth.append(copy)
    for d in (4, 5, 6):
        vec[d].wait_recv()
    ov_ref[...] = vb[...] + v3[0] + v3[1] + v3[2]
    for copy in fourth:
        copy.wait_recv()
    last = remote(fin.at[rows], fin.at[rows], s5.at[0], r5.at[0], twin)
    last.start()
    last.wait_recv()
    o_ref[...] = fin[...].astype(f32)
    last.wait_send()
    for copies in (first, second, third):
        for copy in copies.values():
            copy.wait_send()
    for copy in fourth + vec:
        copy.wait_send()


def sum_call(g, v):
    dma = pltpu.SemaphoreType.DMA
    _, depth, wide = g.shape
    half, cols = depth // 2, wide // 4
    return pl.pallas_call(
        sum_kernel,
        out_shape=[
            jax.ShapeDtypeStruct((depth, wide), f32),
            jax.ShapeDtypeStruct(v.shape, f32),
        ],
        in_specs=[pl.BlockSpec(memory_space=VMEM)] * 2,
        out_specs=[pl.BlockSpec(memory_space=VMEM)] * 2,
        scratch_shapes=[
            VMEM((4, half, wide), bf16),
            VMEM((4, half, wide), bf16),
            VMEM((4, 3, half, cols), bf16),
            VMEM((4, half, cols), bf16),
            VMEM((4, half, cols), bf16),
            VMEM((depth, wide), bf16),
            VMEM(v.shape, f32),
            VMEM(v.shape, f32),
            VMEM((3,) + v.shape, f32),
            VMEM(v.shape, f32),
            VMEM((3,) + v.shape, f32),
            dma((4,)), dma((4,)), dma((12,)), dma((12,)), dma((4,)), dma((4,)),
            dma((4,)), dma((4,)), dma((1,)), dma((1,)), dma((7,)), dma((7,)),
        ],
        compiler_params=pltpu.CompilerParams(
            collective_id=2, has_side_effects=True, vmem_limit_bytes=LIMIT
        ),
        name="gradient_sum",
    )(g, v)


def normed(x):
    average = jnp.mean(x, axis=-1, keepdims=True)
    centered = x - average
    inverse = lax.rsqrt(jnp.mean(centered * centered, axis=-1, keepdims=True) + norm_eps)
    return centered * inverse, inverse


def norm_back(grad, unit, inverse, gain):
    scaled = grad * gain
    return inverse * (
        scaled
        - jnp.mean(scaled, axis=-1, keepdims=True)
        - unit * jnp.mean(scaled * unit, axis=-1, keepdims=True)
    )


def total(x):
    return jnp.sum(x, axis=0, keepdims=True)


def key_present(shape, axis, span, padded, start, valid):
    slot = lax.broadcasted_iota(jnp.int32, shape, axis) + start
    owner = slot // padded
    inside = slot - owner * padded
    return (inside < span) & (owner * span + inside < valid)


def first_kernel(
    span, valid_ref, w_ref, x_all, s_ref, x_ref, oc_ref,
    out_ref, ga_ref, g_ref, v_ref, mc_ref, st_ref, qkv_ref, dq_ref,
    mixed_s, mc_s, prob_s, wr_s,
):
    z = lax.axis_index("grp")
    valid = valid_ref[0]
    n, padded, width = x_all.shape
    depth = w_ref.shape[1]
    hidden = 4 * width
    vec = s_ref[0].astype(f32) + s_ref[1].astype(f32) + s_ref[2].astype(f32) + s_ref[3].astype(f32)
    gain1, bias1, mixb, gain2, bias2, redb = [vec[i : i + 1] for i in range(6)]
    hb_q, hb_v = vec[6:7], vec[7:8]
    expb = jnp.concatenate([vec[8:9], vec[9:10], vec[10:11], vec[11:12]], 1)
    c1, c2, c3 = 3 * width, 4 * width, 8 * width

    w_heads = w_ref[:, :, :c1].reshape(width, c1)
    unit, _ = normed(x_all[...].reshape(n * padded, width).astype(f32))
    low = (unit * gain1 + bias1).astype(bf16)
    proj = dot_nn(low, w_heads)
    qkv_ref[:, :width] = (proj[:, :width] + hb_q).astype(bf16)
    qkv_ref[:, width : 2 * width] = proj[:, width : 2 * width].astype(bf16)
    qkv_ref[:, 2 * width :] = (proj[:, 2 * width :] + hb_v).astype(bf16)
    own = pl.ds(pl.multiple_of(z * padded, 16), padded)
    scale = HEAD_DIM ** (-0.5)
    present = key_present((padded, n * padded), 1, span, padded, 0, valid)
    lses = []
    for head in range(HEADS):
        lo = head * HEAD_DIM
        q = qkv_ref[own, lo : lo + HEAD_DIM]
        k = qkv_ref[:, width + lo : width + lo + HEAD_DIM]
        v = qkv_ref[:, 2 * width + lo : 2 * width + lo + HEAD_DIM]
        scores = jnp.where(present, dot_nt(q, k) * scale, masked_score)
        top = jnp.max(scores, axis=-1, keepdims=True)
        e = jnp.exp(scores - top)
        row = jnp.sum(e, axis=-1, keepdims=True)
        prob = e / row
        prob_s[head] = prob
        lses.append(top + jnp.log(row))
        mixed_s[:, lo : lo + HEAD_DIM] = dot_nn(prob.astype(bf16), v).astype(bf16)
    w_mix = w_ref[:, :, c1:c2].reshape(width, width)
    mixed = mixed_s[...]
    after = x_ref[...].astype(f32) + dot_nn(mixed, w_mix) + mixb
    unit2, inv2 = normed(after)
    low2 = (unit2 * gain2 + bias2).astype(bf16)
    w_exp = w_ref[:, :, c2:c3].reshape(width, hidden)
    pre = dot_nn(low2, w_exp) + expb
    cube = 0.044715
    root = 0.7978845608028654
    t = jnp.tanh(root * (pre + cube * (pre * pre * pre)))
    act = (0.5 * pre * (1.0 + t)).astype(bf16)
    slope = 0.5 * (1.0 + t) + (0.5 * root) * pre * (1.0 - t * t) * (1.0 + (3.0 * cube) * pre * pre)
    for i in range(n):
        for j in range(4):
            lo = i * width + j * depth
            wr_s[lo : lo + depth, :] = w_ref[i, :, c3 + j * width : c3 + (j + 1) * width]
    w_red = wr_s[...]
    out_ref[...] = (after + dot_nn(act, w_red) + redb).astype(bf16)

    oc = oc_ref[...]
    ocf = oc.astype(f32)
    v_ref[...] = jnp.zeros(v_ref.shape, f32)
    v_ref[5:6, :] = total(ocf)
    g_red = dot_tn(act, oc).astype(bf16)
    for i in range(n):
        for j in range(4):
            lo = i * width + j * depth
            g_ref[i, :, c3 + j * width : c3 + (j + 1) * width] = g_red[lo : lo + depth]
    pre_cot = (slope * dot_nt(oc, w_red)).astype(bf16)
    pre_sum = total(pre_cot.astype(f32))
    for i in range(4):
        v_ref[8 + i : 9 + i, :] = pre_sum[:, i * width : (i + 1) * width]
    g_ref[:, :, c2:c3] = dot_tn(low2, pre_cot).astype(bf16).reshape(n, depth, hidden)
    grad2 = dot_nt(pre_cot, w_exp)
    v_ref[3:4, :] = total(grad2 * unit2)
    v_ref[4:5, :] = total(grad2)
    grad_after = ocf + norm_back(grad2, unit2, inv2, gain2)
    ga_ref[...] = grad_after
    attn_cot = grad_after.astype(bf16)
    v_ref[2:3, :] = total(attn_cot.astype(f32))
    g_ref[:, :, c1:c2] = dot_tn(mixed, attn_cot).astype(bf16).reshape(n, depth, width)
    g_ref[:, :, :c1] = jnp.zeros((n, depth, c1), bf16)
    mc_s[...] = dot_nt(attn_cot, w_mix).astype(bf16)
    mc_ref[...] = mc_s[...]
    cols = []
    for head in range(HEADS):
        lo = head * HEAD_DIM
        k = qkv_ref[:, width + lo : width + lo + HEAD_DIM]
        v = qkv_ref[:, 2 * width + lo : 2 * width + lo + HEAD_DIM]
        prob = prob_s[head]
        grad_prob = dot_nt(mc_s[:, lo : lo + HEAD_DIM], v)
        inner = jnp.sum(prob * grad_prob, axis=-1, keepdims=True)
        cols.append(inner)
        score_cot = (prob * (grad_prob - inner)).astype(bf16)
        dq_ref[:, lo : lo + HEAD_DIM] = (dot_nn(score_cot, k) * scale).astype(bf16)
    lane = lax.broadcasted_iota(jnp.int32, (padded, 128), 1)
    stats = jnp.zeros((padded, 128), f32)
    for head in range(HEADS):
        stats = jnp.where(lane == head, lses[head], stats)
        stats = jnp.where(lane == head + 8, cols[head], stats)
    st_ref[...] = stats.T[:ROWS, :]


def first_call(span, valid, w, x_all, s, x, oc):
    n, padded, width = x_all.shape
    shape = jax.ShapeDtypeStruct
    vmem = pl.BlockSpec(memory_space=VMEM)
    return pl.pallas_call(
        functools.partial(first_kernel, span),
        out_shape=[
            shape((padded, width), bf16),
            shape((padded, width), f32),
            shape(w.shape, bf16),
            shape((ROWS, width), f32),
            shape((padded, width), bf16),
            shape((ROWS, padded), f32),
            shape((n * padded, 3 * width), bf16),
            shape((padded, width), bf16),
        ],
        in_specs=[pl.BlockSpec(memory_space=pltpu.SMEM)] + [vmem] * 5,
        out_specs=[vmem] * 8,
        scratch_shapes=[
            VMEM((padded, width), bf16),
            VMEM((padded, width), bf16),
            VMEM((HEADS, padded, n * padded), f32),
            VMEM((4 * width, width), bf16),
        ],
        compiler_params=pltpu.CompilerParams(vmem_limit_bytes=LIMIT),
        name="forward_and_feed_back",
    )(valid, w, x_all, s, x, oc)


def second_kernel(
    span, valid_ref, w_ref, s_ref, x_ref, ga_ref, mc_ref, st_ref, qkv_ref, dq_ref, g_in, v_in,
    ig_ref, g_ref, v_ref, hc_s,
):
    z = lax.axis_index("grp")
    valid = valid_ref[0]
    padded, width = x_ref.shape
    n = mc_ref.shape[0]
    depth = w_ref.shape[1]
    own = pl.ds(pl.multiple_of(z * padded, 16), padded)
    scale = HEAD_DIM ** (-0.5)
    present = key_present((padded, n * padded), 0, span, padded, z * padded, valid)
    hc_s[:, :width] = dq_ref[...]
    for head in range(HEADS):
        lo = head * HEAD_DIM
        q = qkv_ref[:, lo : lo + HEAD_DIM]
        k = qkv_ref[own, width + lo : width + lo + HEAD_DIM]
        v = qkv_ref[own, 2 * width + lo : 2 * width + lo + HEAD_DIM]
        mc = mc_ref[:, :, lo : lo + HEAD_DIM].reshape(n * padded, HEAD_DIM)
        lse = jnp.concatenate([st_ref[i, head : head + 1, :] for i in range(n)], 1)
        inner = jnp.concatenate([st_ref[i, head + 8 : head + 9, :] for i in range(n)], 1)
        prob = jnp.exp(jnp.where(present, dot_nt(k, q) * scale, masked_score) - lse)
        grad_prob = dot_nt(v, mc)
        hc_s[:, 2 * width + lo : 2 * width + lo + HEAD_DIM] = dot_nn(prob.astype(bf16), mc).astype(bf16)
        score_cot = (prob * (grad_prob - inner)).astype(bf16)
        hc_s[:, width + lo : width + lo + HEAD_DIM] = (dot_nn(score_cot, q) * scale).astype(bf16)
    vec = s_ref[0].astype(f32) + s_ref[1].astype(f32) + s_ref[2].astype(f32) + s_ref[3].astype(f32)
    gain1, bias1 = vec[0:1], vec[1:2]
    unit, inverse = normed(x_ref[...].astype(f32))
    low = (unit * gain1 + bias1).astype(bf16)
    hc = hc_s[...]
    v_ref[...] = v_in[...]
    v_ref[6:7, :] = total(hc[:, :width].astype(f32))
    v_ref[7:8, :] = total(hc[:, 2 * width :].astype(f32))
    g_ref[...] = g_in[...]
    g_ref[:, :, : 3 * width] = dot_tn(low, hc).astype(bf16).reshape(n, depth, 3 * width)
    grad = dot_nt(hc, w_ref[:, :, : 3 * width].reshape(width, 3 * width))
    v_ref[0:1, :] = total(grad * unit)
    v_ref[1:2, :] = total(grad)
    ig_ref[...] = ga_ref[...] + norm_back(grad, unit, inverse, gain1)


def second_call(span, valid, w, s, x, ga, mc, st, qkv, dq, g, v):
    padded, width = x.shape
    shape = jax.ShapeDtypeStruct
    vmem = pl.BlockSpec(memory_space=VMEM)
    return pl.pallas_call(
        functools.partial(second_kernel, span),
        out_shape=[shape((padded, width), f32), shape(g.shape, bf16), shape(v.shape, f32)],
        in_specs=[pl.BlockSpec(memory_space=pltpu.SMEM)] + [vmem] * 10,
        out_specs=[vmem] * 3,
        scratch_shapes=[VMEM((padded, 3 * width), bf16)],
        compiler_params=pltpu.CompilerParams(vmem_limit_bytes=LIMIT),
        name="attention_back",
    )(valid, w, s, x, ga, mc, st, qkv, dq, g, v)


def on_device(
    image_tokens, valid_count, first_gain, first_bias, heads_weight, heads_bias,
    mixing_weight, mixing_bias, second_gain, second_bias, expand_weight, expand_bias,
    reduce_weight, reduce_bias, output_cotangent,
):
    _, span, width = image_tokens.shape
    depth = heads_weight.shape[0]
    padded = up(span, 16)
    z = lax.axis_index("grp")

    def pad_rows(x):
        return jnp.pad(x[0], ((0, padded - span), (0, 0)))

    x = pad_rows(image_tokens)
    oc = pad_rows(output_cotangent)
    w = jnp.concatenate(
        [
            heads_weight,
            mixing_weight,
            expand_weight,
            reduce_weight.reshape(4, depth, width).transpose(1, 0, 2).reshape(depth, 4 * width),
        ],
        1,
    )
    ones = jnp.stack([first_gain, first_bias, mixing_bias, second_gain, second_bias, reduce_bias])
    col = jnp.arange(width) // depth == z
    rows6 = jnp.where(col[None, :], jnp.tile(ones, (1, 4)), 0)
    twos = jnp.where(jnp.arange(2 * width) // (2 * depth) == z, jnp.tile(heads_bias, 4), 0)
    fours = jnp.where(jnp.arange(4)[:, None] == z, expand_bias[None, :], 0)
    s = jnp.concatenate(
        [rows6, twos.reshape(2, width), fours, jnp.zeros((ROWS - 12, width), bf16)], 0
    ).astype(bf16)

    w_all, x_all, s_all = gather_call(w, x, s)
    out, ga, g, v, mc, st, qkv, dq = first_call(span, valid_count, w_all, x_all, s_all, x, oc)
    mc_all, st_all = cot_call(mc, st)
    ig, g, v = second_call(span, valid_count, w_all, s_all, x, ga, mc_all, st_all, qkv, dq, g, v)
    g, v = sum_call(g, v)
    teams = lax.axis_size("rep") // TEAM
    if teams > 1:
        g, v = lax.psum((g / TEAM, v / TEAM), "rep")
    six = lax.dynamic_slice(v, (0, z * depth), (6, depth))
    two = lax.dynamic_slice(v[6:8].reshape(2 * width), (z * 2 * depth,), (2 * depth,))
    four = lax.dynamic_slice(v, (8 + z, 0), (1, width))[0]
    c1, c2, c3 = 3 * width, 4 * width, 8 * width
    g_red = g[:, c3:].reshape(depth, 4, width).transpose(1, 0, 2).reshape(4 * depth, width)
    return (
        out[None, :span], ig[None, :span],
        six[0], six[1], g[:, :c1], two, g[:, c1:c2], six[2], six[3], six[4],
        g[:, c2:c3], four, g_red, six[5],
    )


def solution(mesh):
    tokens = P("rep", "grp", None)
    vec, mat = P("grp"), P("grp", None)
    weights = (vec, vec, mat, vec, mat, vec, vec, vec, mat, vec, mat, vec)
    return jax.shard_map(
        on_device,
        mesh=mesh,
        in_specs=(tokens, P("rep")) + weights + (tokens,),
        out_specs=(tokens, tokens) + weights,
        check_vma=False,
    )
```

time: 836 us -> 130 us (0.16)
  blocking collectives: 597 us -> 0 us
  waiting for transfers between devices: 159 us -> 0 us
  Pallas kernels: 0 us -> 109 us
  matrix products: 24.4 us -> 0 us
  between operations: 19.5 us -> 1.61 us
  local copies, waits for them, and re-layouts: 25.5 us -> 16.7 us
    unnamed x3 -> x0, blocking collectives: 509 us -> none
    reduce_scatter x4 -> x0, waiting for transfers between devices: 128 us -> none  [the longest x1 49.8 us: on_device(): lax.psum_scatter(grad_expand_weight, 'grp', scatter_dimension=0, tiled=True)]
    pallas_call x0 -> x5, Pallas kernels: none -> 109 us  [the longest x1 40.1 us: sum_call(): pl.pallas_call(sum_kernel, out_shape=[jax.ShapeDtypeStruct((depth, wide),...]
    all_gather x4 -> x0, blocking collectives: 74.5 us -> none  [the longest x1 25.8 us: on_device(): lax.all_gather(heads_weight, 'grp', axis=0, tiled=True)]
    psum x1 -> x0, waiting for transfers between devices: 29.4 us -> none  [on_device(): lax.psum((group_part[0], group_part[1], group_part[2], group_part[3], gro...]
    dot_general x18 -> x0, matrix products: 24.4 us -> none  [the longest x1 3.26 us: on_device(): jnp.dot(reduce_cot, back_reduce.T, preferred_element_type=f32)]
    unnamed x112 -> x22, local copies, waits for them, and re-layouts: 18.5 us -> 1 us
    psum x1 -> x0, blocking collectives: 12.8 us -> none  [on_device(): lax.psum((group_part[0], group_part[1], group_part[2], group_part[3], gro...]
  transfers between devices with their start and end apart: 7 -> 0, of which waited for: 4 -> 0; matrix products, arithmetic and copies ran while one was open for 5% -> 0% of each run, Pallas kernels for 0% -> 0%
where the time goes in v1:
time: 130 us
  Pallas kernels  109 us (84%)
  local copies, waits for them, and re-layouts  16.7 us (13%)
  other arithmetic  2.77 us (2%)
  between operations  1.61 us (1%)
    pallas_call x1, Pallas kernels, sum_call(): pl.pallas_call(sum_kernel, out_shape=[jax.ShapeDtypeStruct((depth, wide),...  40.1 us
    pallas_call x1, Pallas kernels, gather_call(): pl.pallas_call(gather_kernel, out_shape=[jax.ShapeDtypeStruct((4,) + a.sh...  31.9 us
    pallas_call x1, Pallas kernels, cot_call(): pl.pallas_call(cot_kernel, out_shape=[jax.ShapeDtypeStruct((4,) + a.shape...  15.4 us
    pallas_call x1, Pallas kernels, first_call(): pl.pallas_call(functools.partial(first_kernel, span), out_shape=[shape((p...  12.7 us
    pallas_call x1, Pallas kernels, second_call(): pl.pallas_call(functools.partial(second_kernel, span), out_shape=[shape((...  8.51 us

profile of v1, /device:TPU:0, one launch (start us, length us, event | category | flops | bytes accessed | tf_op | source)
XLA Modules:
  0.0 129.8 jit_solution(8354336548476710195)
XLA Ops:
  0.6 0.0 copy-start
  0.7 0.0 copy-start.2
  0.7 0.0 copy-start.9
  0.7 0.0 copy-start.3
  1.5 1.1 copy.29
  2.6 0.0 copy-start.1
  2.7 2.0 %pad_maximum_fusion.w_ref = bf16[96,4608]{1,0:T(8,128)(2,1)} fusion(bf16[96,1536]{1,0:T(8,128)(2,1)S(1)} %bitcast.31, bf16[96,1536]{1,0:T(8,128)(2,1)} %param.25, bf16[96,384]{1,0:T(8,128)(2,1)} %param.21, bf16[96,1152]{1,0:T(8,128)(2,1)} %param.19), kind=kLoop, calls=%fused_computation | loop fusion | flops 3538944 | bytes 1769472 | tf_op jit(solution)/shard_map/concatenate | solution.py:534
  4.7 0.0 copy-done
  4.7 0.7 pad.7.x_ref
  5.4 0.1 broadcast_select_fusion.1
  5.4 0.1 tile.23
  5.7 0.1 tile.21
  5.8 0.6 pad_maximum_fusion.1.s_ref
  6.4 31.9 %gather.1 = (bf16[4,96,4608]{2,1,0:T(8,128)(2,1)}, bf16[4,160,384]{2,1,0:T(8,128)(2,1)}, bf16[4,16,384]{2,1,0:T(8,128)(2,1)}) custom-call(bf16[96,4608]{1,0:T(8,128)(2,1)} %pad_maximum_fusion.w_ref, bf16[160,384]{1,0:T(8,128)(2,1)} %pad.7.x_ref, bf16[16,384]{1,0:T(8,128)(2,1)} %pad_maximum_fusion.1.s_ref), custom_call_target="tpu_custom_call" | custom-call | tf_op jit(solution)/shard_map/gather/pallas_call | solution.py:132
  38.3 0.7 pad.8.oc_ref
  39.0 12.7 %forward_and_feed_back.1 = (bf16[160,384]{1,0:T(8,128)(2,1)}, f32[160,384]{1,0:T(8,128)}, bf16[4,96,4608]{2,1,0:T(8,128)(2,1)}, f32[16,384]{1,0:T(8,128)}, bf16[...) custom-call(s32[1]{0:T(128)S(6)} %copy.33.valid_ref, ...), custom_call_target="tpu_custom_call" | custom-call | tf_op jit(solution)/shard_map/forward_and_feed_back/pallas_call | solution.py:437
  51.7 1.6 %slice_bitcast_fusion.1 = bf16[1,145,384]{2,1,0:T(8,128)(2,1)} fusion(bf16[160,384]{1,0:T(8,128)(2,1)} %get-tuple-element.35), kind=kLoop, calls=%fused_computation.2 | loop fusion | bytes 222720 | tf_op jit(solution)/shard_map/broadcast_in_dim | solution.py:566
  53.3 15.4 %cotangents.1 = (bf16[4,160,384]{2,1,0:T(8,128)(2,1)}, f32[4,16,160]{2,1,0:T(8,128)}) custom-call(bf16[160,384]{1,0:T(8,128)(2,1)} %get-tuple-element.37.m_ref, f32[16,160]{1,0:T(8,128)} %get-tuple-element.38.t_ref), custom_call_target="tpu_custom_call" | custom-call | tf_op jit(solution)/shard_map/cotangents/pallas_call | solution.py:168
  68.7 8.5 %attention_back.1 = (f32[160,384]{1,0:T(8,128)}, bf16[4,96,4608]{2,1,0:T(8,128)(2,1)}, f32[16,384]{1,0:T(8,128)}) custom-call(s32[1]{0:T(128)S(6)} %copy.33.valid_ref, bf16[4,96,4608]{2,1,0:T(8,128)(2,1)} %get-tuple-element.32.w_ref, bf16[4,16,384]{2,1,0:T(8,128)(2,1)} %get-tuple-element.34.s_ref, bf16[160,384]{1,0:T(8,128)(2,1)} %pad.7.x_ref, ...), custom_call_target="tpu_custom_call" | custom-call | tf_op jit(solution)/shard_map/attention_back/pallas_call | solution.py:508
  77.2 1.0 slice_bitcast_fusion
  78.2 0.9 copy.31
  79.1 40.1 %gradient_sum.1 = (f32[96,4608]{1,0:T(8,128)}, f32[16,384]{1,0:T(8,128)}) custom-call(bf16[4,96,4608]{2,1,0:T(8,128)(2,1)} %get-tuple-element.46.g_ref, f32[16,384]{1,0:T(8,128)} %get-tuple-element.47.v_ref), custom_call_target="tpu_custom_call" | custom-call | tf_op jit(solution)/shard_map/gradient_sum/pallas_call | solution.py:273
  119.2 0.8 constant_dynamic-slice_fusion
  120.0 0.5 slice_bitcast_fusion.2
  120.5 1.8 %slice.43 = f32[96,1152]{1,0:T(8,128)} slice(f32[96,4608]{1,0:T(8,128)} %get-tuple-element.49), slice={[0:96], [0:1152]} | slice | bytes 884736 | tf_op jit(solution)/shard_map/slice | solution.py:567
  122.3 0.7 slice.44
  123.1 0.6 dynamic_slice.10
  123.7 1.6 %slice.45 = f32[96,384]{1,0:T(8,128)} slice(f32[96,4608]{1,0:T(8,128)} %get-tuple-element.49), slice={[0:96], [1152:1536]} | slice | bytes 294912 | tf_op jit(solution)/shard_map/slice | solution.py:567
  125.3 2.1 %fusion.4 = (f32[96,1536]{1,0:T(8,128)S(1)}, f32[96,1536]{1,0:T(8,128)}) fusion(f32[96,4608]{1,0:T(8,128)} %get-tuple-element.49), kind=kLoop, calls=%fused_computation.25 | loop fusion | bytes 2359296 | tf_op jit(solution)/shard_map/slice | solution.py:564
  127.4 1.3 %dynamic-slice_reduce_fusion = f32[384]{0:T(512)} fusion(f32[16,384]{1,0:T(8,128)} %get-tuple-element.48, s32[]{:T(128)S(6)} %select_n.44), kind=kLoop, calls=%fused_computation.16 | loop fusion | bytes 3076 | tf_op jit(solution)/shard_map/dynamic_slice | solution.py:562
  128.7 0.2 reshape.77
  128.9 0.9 copy.30
  (24 shorter events, 0.2 us)
Async XLA Ops:
  0.6 4.0 %copy-start = (bf16[1,145,384]{2,1,0:T(8,128)(2,1)S(1)}, bf16[1,145,384]{2,1,0:T(8,128)(2,1)}, u32[]{:S(2)}) copy-start(bf16[1,145,384]{2,1,0:T(8,128)(2,1)} %param.15) | copy-start | bytes 334084
  0.7 4.7 %copy-start.2 = (bf16[384]{0:T(512)(128)(2,1)S(1)}, bf16[384]{0:T(512)(128)(2,1)}, u32[]{:S(2)}) copy-start(bf16[384]{0:T(512)(128)(2,1)} %param.26) | copy-start | bytes 2308
  0.7 4.8 %copy-start.9 = (bf16[192]{0:T(256)(128)(2,1)S(1)}, bf16[192]{0:T(256)(128)(2,1)}, u32[]{:S(2)}) copy-start(bf16[192]{0:T(256)(128)(2,1)} %param.20) | copy-start | bytes 1156
  0.7 4.9 %copy-start.3 = (bf16[96]{0:T(256)(128)(2,1)S(1)}, bf16[96]{0:T(256)(128)(2,1)}, u32[]{:S(2)}) copy-start(bf16[96]{0:T(256)(128)(2,1)} %param.17) | copy-start | bytes 580
  0.7 4.9 %copy-start.4 = (bf16[96]{0:T(256)(128)(2,1)S(1)}, bf16[96]{0:T(256)(128)(2,1)}, u32[]{:S(2)}) copy-start(bf16[96]{0:T(256)(128)(2,1)} %param.18) | copy-start | bytes 580
  0.7 4.9 %copy-start.5 = (bf16[96]{0:T(256)(128)(2,1)S(1)}, bf16[96]{0:T(256)(128)(2,1)}, u32[]{:S(2)}) copy-start(bf16[96]{0:T(256)(128)(2,1)} %param.22) | copy-start | bytes 580
  0.7 4.9 %copy-start.6 = (bf16[96]{0:T(256)(128)(2,1)S(1)}, bf16[96]{0:T(256)(128)(2,1)}, u32[]{:S(2)}) copy-start(bf16[96]{0:T(256)(128)(2,1)} %param.23) | copy-start | bytes 580
  0.7 4.9 %copy-start.7 = (bf16[96]{0:T(256)(128)(2,1)S(1)}, bf16[96]{0:T(256)(128)(2,1)}, u32[]{:S(2)}) copy-start(bf16[96]{0:T(256)(128)(2,1)} %param.24) | copy-start | bytes 580
  0.7 4.9 %copy-start.8 = (bf16[96]{0:T(256)(128)(2,1)S(1)}, bf16[96]{0:T(256)(128)(2,1)}, u32[]{:S(2)}) copy-start(bf16[96]{0:T(256)(128)(2,1)} %param.28) | copy-start | bytes 580
  2.6 35.7 %copy-start.1 = (bf16[1,145,384]{2,1,0:T(8,128)(2,1)S(1)}, bf16[1,145,384]{2,1,0:T(8,128)(2,1)}, u32[]{:S(2)}) copy-start(bf16[1,145,384]{2,1,0:T(8,128)(2,1)} %param.29) | copy-start | bytes 334084

commit v2 on v1

--- a/solution.py
+++ b/solution.py
@@ -70,19 +70,26 @@
 
 
 def gather_kernel(
-    w_ref, x_ref, s_ref, w_all, x_all, s_all,
+    wh_ref, wm_ref, we_ref, wr_ref, x_ref, s_ref, w_all, x_all, s_all,
     zs, zr, xs, xr, ss, sr, ps, pr, cs, cr, loc,
 ):
     rep, z, core, spot, base = places()
     over_z, plane, twin = team_devices()
-    half = w_ref.shape[0] // 2
-    cols = w_ref.shape[1] // 4
+    half = w_all.shape[1] // 2
+    cols = w_all.shape[2] // 4
     rows = pl.ds(pl.multiple_of(core * half, 16), half)
     part = pl.ds(pl.multiple_of(spot * cols, 128), cols)
+    depth, width = wm_ref.shape
+    c1, c2, c3 = 3 * width, 4 * width, 8 * width
+    w_all[z, :, :c1] = wh_ref[...]
+    w_all[z, :, c1:c2] = wm_ref[...]
+    w_all[z, :, c2:c3] = we_ref[...]
+    for j in range(4):
+        w_all[z, :, c3 + j * width : c3 + (j + 1) * width] = wr_ref[j * depth : (j + 1) * depth, :]
     greet(over_z + plane + [twin])
     copies = []
     for d in (1, 2, 3):
-        copy = remote(w_ref.at[rows, part], w_all.at[z, rows, part], zs.at[d], zr.at[d], over_z[d - 1])
+        copy = remote(w_all.at[z, rows, part], w_all.at[z, rows, part], zs.at[d], zr.at[d], over_z[d - 1])
         copy.start()
         copies.append(copy)
     others = []
@@ -93,7 +100,7 @@
         b.start()
         others += [a, b]
     locals_ = []
-    for k, (src, dst) in enumerate(((w_ref, w_all), (x_ref, x_all), (s_ref, s_all))):
+    for k, (src, dst) in enumerate(((x_ref, x_all), (s_ref, s_all))):
         copy = pltpu.make_async_copy(src, dst.at[z], loc.at[k])
         copy.start()
         locals_.append(copy)
@@ -127,177 +134,122 @@
         copy.wait()
 
 
-def gather_call(w, x, s):
+def gather_call(weights, x, s):
     dma = pltpu.SemaphoreType.DMA
+    depth, width = weights[1].shape
     return pl.pallas_call(
         gather_kernel,
-        out_shape=[jax.ShapeDtypeStruct((4,) + a.shape, a.dtype) for a in (w, x, s)],
-        in_specs=[pl.BlockSpec(memory_space=VMEM)] * 3,
+        out_shape=[
+            jax.ShapeDtypeStruct((4, depth, 12 * width), bf16),
+            jax.ShapeDtypeStruct((4,) + x.shape, bf16),
+            jax.ShapeDtypeStruct((4,) + s.shape, bf16),
+        ],
+        in_specs=[pl.BlockSpec(memory_space=VMEM)] * 6,
         out_specs=[pl.BlockSpec(memory_space=VMEM)] * 3,
-        scratch_shapes=[dma((4,))] * 6 + [dma((9,))] * 2 + [dma((4,))] * 2 + [dma((3,))],
+        scratch_shapes=[dma((4,))] * 6 + [dma((9,))] * 2 + [dma((4,))] * 2 + [dma((2,))],
         compiler_params=pltpu.CompilerParams(
             collective_id=0, has_side_effects=True, vmem_limit_bytes=LIMIT
         ),
         name="gather",
-    )(w, x, s)
-
-
-def cot_kernel(m_ref, t_ref, m_all, t_all, ms, mr, ts, tr, loc):
-    rep, z, core, spot, base = places()
-    over_z, _, _ = team_devices()
-    greet(over_z)
-    sent = []
-    for d in (1, 2, 3):
-        a = remote(m_ref, m_all.at[z], ms.at[d], mr.at[d], over_z[d - 1])
-        b = remote(t_ref, t_all.at[z], ts.at[d], tr.at[d], over_z[d - 1])
-        a.start()
-        b.start()
-        sent += [a, b]
-    c = pltpu.make_async_copy(m_ref, m_all.at[z], loc.at[0])
-    e = pltpu.make_async_copy(t_ref, t_all.at[z], loc.at[1])
-    c.start()
-    e.start()
-    c.wait()
-    e.wait()
-    for copy in sent:
-        copy.wait()
-
-
-def cot_call(m, t):
+    )(*weights, x, s)
+
+
+class Flow:
+    def __init__(self, g, got1, h, got2, mine, got3, fin, s1, r1, s2, r2, s3, r3, s4, r4, s5, r5):
+        self.__dict__.update(locals())
+        rep, self.z, self.core, self.spot, base = places()
+        self.over_z, self.plane, self.twin = team_devices()
+        half = g.shape[1] // 2
+        self.cols = g.shape[2] // 4
+        self.rows = pl.ds(pl.multiple_of(self.core * half, 16), half)
+        self.away = pl.ds(pl.multiple_of((1 - self.core) * half, 16), half)
+        self.order = (2, 1, 3, 0)
+        self.sent = []
+
+    def part(self, index):
+        return pl.ds(pl.multiple_of(index * self.cols, 128), self.cols)
+
+    def go(self, *args):
+        copy = remote(*args)
+        copy.start()
+        self.sent.append(copy)
+        return copy
+
+    def to_twin(self):
+        self.first = {}
+        for d in self.order:
+            to = lax.rem(self.z + d, 4)
+            self.first[d] = self.go(
+                self.g.at[to, self.away], self.got1.at[d], self.s1.at[d], self.r1.at[d], self.twin
+            )
+
+    def to_plane(self):
+        self.second = {}
+        for d in self.order:
+            to = lax.rem(self.z + d, 4)
+            self.first[d].wait_recv()
+            both = self.g[to, self.rows, :].astype(f32) + self.got1[d].astype(f32)
+            self.h[d] = both.astype(bf16)
+            for e in (1, 2, 3):
+                there = lax.rem(self.spot + e, 4)
+                k = d * 3 + e - 1
+                self.second[d, e] = self.go(
+                    self.h.at[d, :, self.part(there)], self.got2.at[d, e - 1],
+                    self.s2.at[k], self.r2.at[k], self.plane[e - 1],
+                )
+
+    def to_group(self):
+        self.third = {}
+        for d in self.order:
+            summed = self.h[d, :, self.part(self.spot)].astype(f32)
+            for e in (1, 2, 3):
+                self.second[d, e].wait_recv()
+                summed += self.got2[d, e - 1].astype(f32)
+            self.mine[d] = summed.astype(bf16)
+            if d:
+                self.third[d] = self.go(
+                    self.mine.at[d], self.got3.at[d], self.s3.at[d], self.r3.at[d], self.over_z[d - 1]
+                )
+
+    def spread(self):
+        summed = self.mine[0].astype(f32)
+        for d in (1, 2, 3):
+            self.third[d].wait_recv()
+            summed += self.got3[d].astype(f32)
+        here = (self.rows, self.part(self.spot))
+        self.fin[here] = summed.astype(bf16)
+        self.fourth = []
+        for e in (1, 2, 3):
+            self.fourth.append(
+                self.go(self.fin.at[here], self.fin.at[here], self.s4.at[e], self.r4.at[e], self.plane[e - 1])
+            )
+
+    def cross(self):
+        for copy in self.fourth:
+            copy.wait_recv()
+        self.last = self.go(
+            self.fin.at[self.rows], self.fin.at[self.rows], self.s5.at[0], self.r5.at[0], self.twin
+        )
+
+    def finish(self):
+        self.last.wait_recv()
+        for copy in self.sent:
+            copy.wait_send()
+
+
+def flow_scratch(depth, wide):
     dma = pltpu.SemaphoreType.DMA
-    return pl.pallas_call(
-        cot_kernel,
-        out_shape=[jax.ShapeDtypeStruct((4,) + a.shape, a.dtype) for a in (m, t)],
-        in_specs=[pl.BlockSpec(memory_space=VMEM)] * 2,
-        out_specs=[pl.BlockSpec(memory_space=VMEM)] * 2,
-        scratch_shapes=[dma((4,))] * 4 + [dma((2,))],
-        compiler_params=pltpu.CompilerParams(
-            collective_id=1, has_side_effects=True, vmem_limit_bytes=LIMIT
-        ),
-        name="cotangents",
-    )(m, t)
-
-
-def sum_kernel(
-    g_ref, v_ref, o_ref, ov_ref,
-    got1, h, got2, mine, got3, fin, v1, va, v2, vb, v3,
-    s1, r1, s2, r2, s3, r3, s4, r4, s5, r5, sv, rv,
-):
-    rep, z, core, spot, base = places()
-    over_z, plane, twin = team_devices()
-    half = g_ref.shape[1] // 2
-    cols = g_ref.shape[2] // 4
-    rows = pl.ds(pl.multiple_of(core * half, 16), half)
-    away = pl.ds(pl.multiple_of((1 - core) * half, 16), half)
-
-    def part(index):
-        return pl.ds(pl.multiple_of(index * cols, 128), cols)
-
-    greet(over_z + plane + [twin])
-    order = (2, 1, 3, 0)
-    first = {}
-    for d in order:
-        to = lax.rem(z + d, 4)
-        copy = remote(g_ref.at[to, away], got1.at[d], s1.at[d], r1.at[d], twin)
-        copy.start()
-        first[d] = copy
-    vec = [remote(v_ref, v1, sv.at[0], rv.at[0], twin)]
-    vec[0].start()
-    second = {}
-    for d in order:
-        to = lax.rem(z + d, 4)
-        first[d].wait_recv()
-        h[d] = (g_ref[to, rows, :].astype(f32) + got1[d].astype(f32)).astype(bf16)
-        for e in (1, 2, 3):
-            there = lax.rem(spot + e, 4)
-            copy = remote(h.at[d, :, part(there)], got2.at[d, e - 1],
-                          s2.at[d * 3 + e - 1], r2.at[d * 3 + e - 1], plane[e - 1])
-            copy.start()
-            second[d, e] = copy
-    vec[0].wait_recv()
-    va[...] = v_ref[...] + v1[...]
-    for e in (1, 2, 3):
-        copy = remote(va, v2.at[e - 1], sv.at[e], rv.at[e], plane[e - 1])
-        copy.start()
-        vec.append(copy)
-    third = {}
-    for d in order:
-        total = h[d, :, part(spot)].astype(f32)
-        for e in (1, 2, 3):
-            second[d, e].wait_recv()
-            total += got2[d, e - 1].astype(f32)
-        mine[d] = total.astype(bf16)
-        if d:
-            copy = remote(mine.at[d], got3.at[d], s3.at[d], r3.at[d], over_z[d - 1])
-            copy.start()
-            third[d] = copy
-    for e in (1, 2, 3):
-        vec[e].wait_recv()
-    vb[...] = va[...] + v2[0] + v2[1] + v2[2]
-    for d in (1, 2, 3):
-        copy = remote(vb, v3.at[d - 1], sv.at[d + 3], rv.at[d + 3], over_z[d - 1])
-        copy.start()
-        vec.append(copy)
-    total = mine[0].astype(f32)
-    for d in (1, 2, 3):
-        third[d].wait_recv()
-        total += got3[d].astype(f32)
-    fin[rows, part(spot)] = total.astype(bf16)
-    fourth = []
-    for e in (1, 2, 3):
-        here = fin.at[rows, part(spot)]
-        copy = remote(here, here, s4.at[e], r4.at[e], plane[e - 1])
-        copy.start()
-        fourth.append(copy)
-    for d in (4, 5, 6):
-        vec[d].wait_recv()
-    ov_ref[...] = vb[...] + v3[0] + v3[1] + v3[2]
-    for copy in fourth:
-        copy.wait_recv()
-    last = remote(fin.at[rows], fin.at[rows], s5.at[0], r5.at[0], twin)
-    last.start()
-    last.wait_recv()
-    o_ref[...] = fin[...].astype(f32)
-    last.wait_send()
-    for copies in (first, second, third):
-        for copy in copies.values():
-            copy.wait_send()
-    for copy in fourth + vec:
-        copy.wait_send()
-
-
-def sum_call(g, v):
-    dma = pltpu.SemaphoreType.DMA
-    _, depth, wide = g.shape
     half, cols = depth // 2, wide // 4
-    return pl.pallas_call(
-        sum_kernel,
-        out_shape=[
-            jax.ShapeDtypeStruct((depth, wide), f32),
-            jax.ShapeDtypeStruct(v.shape, f32),
-        ],
-        in_specs=[pl.BlockSpec(memory_space=VMEM)] * 2,
-        out_specs=[pl.BlockSpec(memory_space=VMEM)] * 2,
-        scratch_shapes=[
-            VMEM((4, half, wide), bf16),
-            VMEM((4, half, wide), bf16),
-            VMEM((4, 3, half, cols), bf16),
-            VMEM((4, half, cols), bf16),
-            VMEM((4, half, cols), bf16),
-            VMEM((depth, wide), bf16),
-            VMEM(v.shape, f32),
-            VMEM(v.shape, f32),
-            VMEM((3,) + v.shape, f32),
-            VMEM(v.shape, f32),
-            VMEM((3,) + v.shape, f32),
-            dma((4,)), dma((4,)), dma((12,)), dma((12,)), dma((4,)), dma((4,)),
-            dma((4,)), dma((4,)), dma((1,)), dma((1,)), dma((7,)), dma((7,)),
-        ],
-        compiler_params=pltpu.CompilerParams(
-            collective_id=2, has_side_effects=True, vmem_limit_bytes=LIMIT
-        ),
-        name="gradient_sum",
-    )(g, v)
+    return [
+        VMEM((4, half, wide), bf16),
+        VMEM((4, half, wide), bf16),
+        VMEM((4, 3, half, cols), bf16),
+        VMEM((4, half, cols), bf16),
+        VMEM((4, half, cols), bf16),
+    ], [
+        dma((4,)), dma((4,)), dma((12,)), dma((12,)), dma((4,)), dma((4,)),
+        dma((4,)), dma((4,)), dma((1,)), dma((1,)),
+    ]
 
 
 def normed(x):
@@ -329,7 +281,7 @@
 
 def first_kernel(
     span, valid_ref, w_ref, x_all, s_ref, x_ref, oc_ref,
-    out_ref, ga_ref, g_ref, v_ref, mc_ref, st_ref, qkv_ref, dq_ref,
+    out_ref, ga_ref, g_ref, gm_ref, v_ref, mc_ref, st_ref, qkv_ref, dq_ref,
     mixed_s, mc_s, prob_s, wr_s,
 ):
     z = lax.axis_index("grp")
@@ -394,12 +346,12 @@
     for i in range(n):
         for j in range(4):
             lo = i * width + j * depth
-            g_ref[i, :, c3 + j * width : c3 + (j + 1) * width] = g_red[lo : lo + depth]
+            g_ref[i, :, c2 + j * width : c2 + (j + 1) * width] = g_red[lo : lo + depth]
     pre_cot = (slope * dot_nt(oc, w_red)).astype(bf16)
     pre_sum = total(pre_cot.astype(f32))
     for i in range(4):
         v_ref[8 + i : 9 + i, :] = pre_sum[:, i * width : (i + 1) * width]
-    g_ref[:, :, c2:c3] = dot_tn(low2, pre_cot).astype(bf16).reshape(n, depth, hidden)
+    g_ref[:, :, :c2] = dot_tn(low2, pre_cot).astype(bf16).reshape(n, depth, hidden)
     grad2 = dot_nt(pre_cot, w_exp)
     v_ref[3:4, :] = total(grad2 * unit2)
     v_ref[4:5, :] = total(grad2)
@@ -407,8 +359,7 @@
     ga_ref[...] = grad_after
     attn_cot = grad_after.astype(bf16)
     v_ref[2:3, :] = total(attn_cot.astype(f32))
-    g_ref[:, :, c1:c2] = dot_tn(mixed, attn_cot).astype(bf16).reshape(n, depth, width)
-    g_ref[:, :, :c1] = jnp.zeros((n, depth, c1), bf16)
+    gm_ref[...] = dot_tn(mixed, attn_cot).astype(bf16).reshape(n, depth, width)
     mc_s[...] = dot_nt(attn_cot, w_mix).astype(bf16)
     mc_ref[...] = mc_s[...]
     cols = []
@@ -439,7 +390,8 @@
         out_shape=[
             shape((padded, width), bf16),
             shape((padded, width), f32),
-            shape(w.shape, bf16),
+            shape((n, w.shape[1], 8 * width), bf16),
+            shape((n, w.shape[1], width), bf16),
             shape((ROWS, width), f32),
             shape((padded, width), bf16),
             shape((ROWS, padded), f32),
@@ -447,7 +399,7 @@
             shape((padded, width), bf16),
         ],
         in_specs=[pl.BlockSpec(memory_space=pltpu.SMEM)] + [vmem] * 5,
-        out_specs=[vmem] * 8,
+        out_specs=[vmem] * 9,
         scratch_shapes=[
             VMEM((padded, width), bf16),
             VMEM((padded, width), bf16),
@@ -460,18 +412,39 @@
 
 
 def second_kernel(
-    span, valid_ref, w_ref, s_ref, x_ref, ga_ref, mc_ref, st_ref, qkv_ref, dq_ref, g_in, v_in,
-    ig_ref, g_ref, v_ref, hc_s,
+    span, valid_ref, w_ref, s_ref, x_ref, ga_ref, mc_in, st_in, qkv_ref, dq_ref, g_in, gm_ref, v_in,
+    ig_ref, fa_ref, fb_ref, ov_ref, *scratch,
 ):
+    hc_s, mc_ref, st_ref, gb, v_ref, v1, va, v2, vb, v3, ms, mr, ts, tr, sv, rv = scratch[:16]
+    fa = Flow(g_in, *scratch[16:21], fa_ref, *scratch[21:31])
+    fb = Flow(gb, *scratch[31:36], fb_ref, *scratch[36:46])
     z = lax.axis_index("grp")
+    over_z, plane, twin = team_devices()
     valid = valid_ref[0]
     padded, width = x_ref.shape
     n = mc_ref.shape[0]
     depth = w_ref.shape[1]
+    greet(over_z + plane + [twin])
+    cots = []
+    for d in (1, 2, 3):
+        a = remote(mc_in, mc_ref.at[z], ms.at[d], mr.at[d], over_z[d - 1])
+        b = remote(st_in, st_ref.at[z], ts.at[d], tr.at[d], over_z[d - 1])
+        a.start()
+        b.start()
+        cots += [a, b]
+    fa.to_twin()
+    mc_ref[z] = mc_in[...]
+    st_ref[z] = st_in[...]
+    hc_s[:, :width] = dq_ref[...]
+    gb[:, :, 3 * width :] = gm_ref[...]
+    vec = s_ref[0].astype(f32) + s_ref[1].astype(f32) + s_ref[2].astype(f32) + s_ref[3].astype(f32)
+    gain1, bias1 = vec[0:1], vec[1:2]
+    fa.to_plane()
+    for copy in cots:
+        copy.wait()
     own = pl.ds(pl.multiple_of(z * padded, 16), padded)
     scale = HEAD_DIM ** (-0.5)
     present = key_present((padded, n * padded), 0, span, padded, z * padded, valid)
-    hc_s[:, :width] = dq_ref[...]
     for head in range(HEADS):
         lo = head * HEAD_DIM
         q = qkv_ref[:, lo : lo + HEAD_DIM]
@@ -485,35 +458,110 @@
         hc_s[:, 2 * width + lo : 2 * width + lo + HEAD_DIM] = dot_nn(prob.astype(bf16), mc).astype(bf16)
         score_cot = (prob * (grad_prob - inner)).astype(bf16)
         hc_s[:, width + lo : width + lo + HEAD_DIM] = (dot_nn(score_cot, q) * scale).astype(bf16)
-    vec = s_ref[0].astype(f32) + s_ref[1].astype(f32) + s_ref[2].astype(f32) + s_ref[3].astype(f32)
-    gain1, bias1 = vec[0:1], vec[1:2]
     unit, inverse = normed(x_ref[...].astype(f32))
     low = (unit * gain1 + bias1).astype(bf16)
     hc = hc_s[...]
+    gb[:, :, : 3 * width] = dot_tn(low, hc).astype(bf16).reshape(n, depth, 3 * width)
+    fb.to_twin()
     v_ref[...] = v_in[...]
     v_ref[6:7, :] = total(hc[:, :width].astype(f32))
     v_ref[7:8, :] = total(hc[:, 2 * width :].astype(f32))
-    g_ref[...] = g_in[...]
-    g_ref[:, :, : 3 * width] = dot_tn(low, hc).astype(bf16).reshape(n, depth, 3 * width)
     grad = dot_nt(hc, w_ref[:, :, : 3 * width].reshape(width, 3 * width))
     v_ref[0:1, :] = total(grad * unit)
     v_ref[1:2, :] = total(grad)
+    vecs = [remote(v_ref, v1, sv.at[0], rv.at[0], twin)]
+    vecs[0].start()
+    fb.to_plane()
+    fa.to_group()
     ig_ref[...] = ga_ref[...] + norm_back(grad, unit, inverse, gain1)
-
-
-def second_call(span, valid, w, s, x, ga, mc, st, qkv, dq, g, v):
+    vecs[0].wait_recv()
+    va[...] = v_ref[...] + v1[...]
+    for e in (1, 2, 3):
+        copy = remote(va, v2.at[e - 1], sv.at[e], rv.at[e], plane[e - 1])
+        copy.start()
+        vecs.append(copy)
+    fb.to_group()
+    for e in (1, 2, 3):
+        vecs[e].wait_recv()
+    vb[...] = va[...] + v2[0] + v2[1] + v2[2]
+    for d in (1, 2, 3):
+        copy = remote(vb, v3.at[d - 1], sv.at[d + 3], rv.at[d + 3], over_z[d - 1])
+        copy.start()
+        vecs.append(copy)
+    fa.spread()
+    fb.spread()
+    fa.cross()
+    fb.cross()
+    for d in (4, 5, 6):
+        vecs[d].wait_recv()
+    ov_ref[...] = vb[...] + v3[0] + v3[1] + v3[2]
+    fa.finish()
+    fb.finish()
+    for copy in vecs:
+        copy.wait_send()
+
+
+def second_call(span, valid, w, s, x, ga, mc, st, qkv, dq, g, gm, v):
     padded, width = x.shape
+    depth = w.shape[1]
+    shape = jax.ShapeDtypeStruct
+    vmem = pl.BlockSpec(memory_space=VMEM)
+    dma = pltpu.SemaphoreType.DMA
+    bufs_a, sems_a = flow_scratch(depth, 8 * width)
+    bufs_b, sems_b = flow_scratch(depth, 4 * width)
+    return pl.pallas_call(
+        functools.partial(second_kernel, span),
+        out_shape=[
+            shape((padded, width), f32), shape((depth, 8 * width), bf16),
+            shape((depth, 4 * width), bf16), shape(v.shape, f32),
+        ],
+        in_specs=[pl.BlockSpec(memory_space=pltpu.SMEM)] + [vmem] * 11,
+        out_specs=[vmem] * 4,
+        scratch_shapes=[
+            VMEM((padded, 3 * width), bf16),
+            VMEM((4,) + mc.shape, bf16),
+            VMEM((4,) + st.shape, f32),
+            VMEM((4, depth, 4 * width), bf16),
+            VMEM(v.shape, f32),
+            VMEM(v.shape, f32),
+            VMEM(v.shape, f32),
+            VMEM((3,) + v.shape, f32),
+            VMEM(v.shape, f32),
+            VMEM((3,) + v.shape, f32),
+            dma((4,)), dma((4,)), dma((4,)), dma((4,)), dma((7,)), dma((7,)),
+        ] + bufs_a + sems_a + bufs_b + sems_b,
+        compiler_params=pltpu.CompilerParams(
+            collective_id=1, has_side_effects=True, vmem_limit_bytes=LIMIT
+        ),
+        name="attention_back_and_sum",
+    )(valid, w, s, x, ga, mc, st, qkv, dq, g, gm, v)
+
+
+def unpack_kernel(a_ref, b_ref, h_ref, m_ref, e_ref, r_ref):
+    depth, width = m_ref.shape
+    h_ref[...] = b_ref[:, : 3 * width].astype(f32)
+    m_ref[...] = b_ref[:, 3 * width :].astype(f32)
+    e_ref[...] = a_ref[:, : 4 * width].astype(f32)
+    for j in range(4):
+        lo = (4 + j) * width
+        r_ref[j * depth : (j + 1) * depth, :] = a_ref[:, lo : lo + width].astype(f32)
+
+
+def unpack_call(a, b):
+    depth, width = a.shape[0], a.shape[1] // 8
     shape = jax.ShapeDtypeStruct
     vmem = pl.BlockSpec(memory_space=VMEM)
     return pl.pallas_call(
-        functools.partial(second_kernel, span),
-        out_shape=[shape((padded, width), f32), shape(g.shape, bf16), shape(v.shape, f32)],
-        in_specs=[pl.BlockSpec(memory_space=pltpu.SMEM)] + [vmem] * 10,
-        out_specs=[vmem] * 3,
-        scratch_shapes=[VMEM((padded, 3 * width), bf16)],
+        unpack_kernel,
+        out_shape=[
+            shape((depth, 3 * width), f32), shape((depth, width), f32),
+            shape((depth, 4 * width), f32), shape((4 * depth, width), f32),
+        ],
+        in_specs=[vmem] * 2,
+        out_specs=[vmem] * 4,
         compiler_params=pltpu.CompilerParams(vmem_limit_bytes=LIMIT),
-        name="attention_back",
-    )(valid, w, s, x, ga, mc, st, qkv, dq, g, v)
+        name="unpack",
+    )(a, b)
 
 
 def on_device(
@@ -531,15 +579,6 @@
 
     x = pad_rows(image_tokens)
     oc = pad_rows(output_cotangent)
-    w = jnp.concatenate(
-        [
-            heads_weight,
-            mixing_weight,
-            expand_weight,
-            reduce_weight.reshape(4, depth, width).transpose(1, 0, 2).reshape(depth, 4 * width),
-        ],
-        1,
-    )
     ones = jnp.stack([first_gain, first_bias, mixing_bias, second_gain, second_bias, reduce_bias])
     col = jnp.arange(width) // depth == z
     rows6 = jnp.where(col[None, :], jnp.tile(ones, (1, 4)), 0)
@@ -549,23 +588,25 @@
         [rows6, twos.reshape(2, width), fours, jnp.zeros((ROWS - 12, width), bf16)], 0
     ).astype(bf16)
 
-    w_all, x_all, s_all = gather_call(w, x, s)
-    out, ga, g, v, mc, st, qkv, dq = first_call(span, valid_count, w_all, x_all, s_all, x, oc)
-    mc_all, st_all = cot_call(mc, st)
-    ig, g, v = second_call(span, valid_count, w_all, s_all, x, ga, mc_all, st_all, qkv, dq, g, v)
-    g, v = sum_call(g, v)
+    weights = (heads_weight, mixing_weight, expand_weight, reduce_weight)
+    w_all, x_all, s_all = gather_call(weights, x, s)
+    out, ga, g, gm, v, mc, st, qkv, dq = first_call(span, valid_count, w_all, x_all, s_all, x, oc)
+    ig, ga_sum, gb_sum, v = second_call(
+        span, valid_count, w_all, s_all, x, ga, mc, st, qkv, dq, g, gm, v
+    )
     teams = lax.axis_size("rep") // TEAM
     if teams > 1:
-        g, v = lax.psum((g / TEAM, v / TEAM), "rep")
+        ga_sum, gb_sum, v = lax.psum(
+            (ga_sum.astype(f32) / TEAM, gb_sum.astype(f32) / TEAM, v / TEAM), "rep"
+        )
+    g_heads, g_mix, g_exp, g_red = unpack_call(ga_sum, gb_sum)
     six = lax.dynamic_slice(v, (0, z * depth), (6, depth))
     two = lax.dynamic_slice(v[6:8].reshape(2 * width), (z * 2 * depth,), (2 * depth,))
     four = lax.dynamic_slice(v, (8 + z, 0), (1, width))[0]
-    c1, c2, c3 = 3 * width, 4 * width, 8 * width
-    g_red = g[:, c3:].reshape(depth, 4, width).transpose(1, 0, 2).reshape(4 * depth, width)
     return (
         out[None, :span], ig[None, :span],
-        six[0], six[1], g[:, :c1], two, g[:, c1:c2], six[2], six[3], six[4],
-        g[:, c2:c3], four, g_red, six[5],
+        six[0], six[1], g_heads, two, g_mix, six[2], six[3], six[4],
+        g_exp, four, g_red, six[5],
     )
 
 

time: 130 us -> 104 us (0.80)
  Pallas kernels: 109 us -> 88.3 us
  local copies, waits for them, and re-layouts: 16.7 us -> 12.1 us
  other arithmetic: 2.77 us -> 1.42 us
    pallas_call x3 -> x2, Pallas kernels: 87.4 us -> 34.4 us  [the longest x1 32 us: gather_call(): pl.pallas_call(gather_kernel, out_shape=[jax.ShapeDtypeStruct((4, depth,...]
    pallas_call x1, Pallas kernels: 8.51 us -> 41 us  [second_call(): pl.pallas_call(functools.partial(second_kernel, span), out_shape=[shape((...]
    slice x3 -> x0, local copies, waits for them, and re-layouts: 5.51 us -> none  [the longest x1 2.13 us: on_device(): g[:, c3:].reshape(depth, 4, width).transpose(1, 0, 2)]
    concatenate x1 -> x0, other arithmetic: 2.03 us -> none  [on_device(): jnp.concatenate([heads_weight, mixing_weight, expand_weight, reduce_weigh...]
    pad x2, local copies, waits for them, and re-layouts: 1.33 us -> 3.13 us  [pad_rows(): return jnp.pad(x[0], ((0, padded - span), (0, 0)))]
    reshape x2 -> x0, local copies, waits for them, and re-layouts: 1.32 us -> none  [the longest x1 1.12 us: on_device(): reduce_weight.reshape(4, depth, width).transpose(1, 0, 2)]
where the time goes in v2:
time: 104 us; the launch traced here: 103 us
  Pallas kernels  88.3 us (85%)
  local copies, waits for them, and re-layouts  12.1 us (12%)
  other arithmetic  1.42 us (1%)
  between operations  1.34 us (1%)
    pallas_call x1, Pallas kernels, second_call(): pl.pallas_call(functools.partial(second_kernel, span), out_shape=[shape((...  41 us
    pallas_call x1, Pallas kernels, gather_call(): pl.pallas_call(gather_kernel, out_shape=[jax.ShapeDtypeStruct((4, depth,...  32 us
    pallas_call x1, Pallas kernels, first_call(): pl.pallas_call(functools.partial(first_kernel, span), out_shape=[shape((p...  12.9 us
    pad x2, local copies, waits for them, and re-layouts, pad_rows(): return jnp.pad(x[0], ((0, padded - span), (0, 0)))  3.13 us
    pallas_call x1, Pallas kernels, unpack_call(): pl.pallas_call(unpack_kernel, out_shape=[shape((depth, 3 * width), f32),...  2.35 us

profile of v2, /device:TPU:0, one launch (start us, length us, event | category | flops | bytes accessed | tf_op | source)
XLA Modules:
  0.0 103.2 jit_solution(4711694355713979743)
XLA Ops:
  1.3 1.6 %pad.7.x_ref = bf16[160,384]{1,0:T(8,128)(2,1)} pad(bf16[145,384]{1,0:T(8,128)(2,1)} %bitcast.24, bf16[]{:T(256)} %constant.30.clone.1), padding=0_15x0_0 | pad | bytes 234242 | tf_op jit(solution)/shard_map/jit(_pad)/pad | solution.py:578
  2.9 0.8 broadcast_select_fusion.1
  3.6 0.7 tile.22
  4.3 0.1 tile.23
  4.4 0.8 stack.27
  5.2 0.1 tile.21
  5.3 0.6 pad_maximum_fusion.s_ref
  5.9 32.0 %gather.1 = (bf16[4,96,4608]{2,1,0:T(8,128)(2,1)}, bf16[4,160,384]{2,1,0:T(8,128)(2,1)}, bf16[4,16,384]{2,1,0:T(8,128)(2,1)}) custom-call(bf16[96,1152]{1,0:T(8,128)(2,1)} %wh_ref.1, bf16[96,384]{1,0:T(8,128)(2,1)} %wm_ref.1, bf16[96,1536]{1,0:T(8,128)(2,1)} %we_ref.1, bf16[384,384]{1,0:T(8,128)(2,1)} %wr_ref.1, bf16[160,384]{1,0:T(8,128)(2,1)} %pad.7.x_ref, ...), custom_call_target="tpu_custom_call" | custom-call | tf_op jit(solution)/shard_map/gather/pallas_call | solution.py:140
  37.9 1.6 %pad.8.oc_ref = bf16[160,384]{1,0:T(8,128)(2,1)} pad(bf16[145,384]{1,0:T(8,128)(2,1)} %bitcast.25, bf16[]{:T(256)} %constant.30.clone.1), padding=0_15x0_0 | pad | bytes 234242 | tf_op jit(solution)/shard_map/jit(_pad)/pad | solution.py:578
  39.5 12.9 %forward_and_feed_back.1 = (bf16[160,384]{1,0:T(8,128)(2,1)}, f32[160,384]{1,0:T(8,128)}, bf16[4,96,3072]{2,1,0:T(8,128)(2,1)}, bf16[4,96,384]{2,1,0:T(8,128)(2,...) custom-call(s32[1]{0:T(128)S(6)} %copy.30.valid_ref, ...), custom_call_target="tpu_custom_call" | custom-call | tf_op jit(solution)/shard_map/forward_and_feed_back/pallas_call | solution.py:388
  52.5 1.6 %slice_bitcast_fusion.1 = bf16[1,145,384]{2,1,0:T(8,128)(2,1)} fusion(bf16[160,384]{1,0:T(8,128)(2,1)} %get-tuple-element.37), kind=kLoop, calls=%fused_computation.1 | loop fusion | bytes 222720 | tf_op jit(solution)/shard_map/broadcast_in_dim | solution.py:607
  54.0 41.0 %attention_back_and_sum.1 = (f32[160,384]{1,0:T(8,128)}, bf16[96,3072]{1,0:T(8,128)(2,1)}, bf16[96,1536]{1,0:T(8,128)(2,1)}, f32[16,384]{1,0:T(8,128)}) custom-call(s32[1]{0:T(128)S(6)} %copy.30.valid_ref, bf16[4,96,4608]{2,1,0:T(8,128)(2,1)} %get-tuple-element.34.w_ref, bf16[4,16,384]{2,1,0:T(8,128)(2,1)} %get-tuple-element.36.s_ref, ...), custom_call_target="tpu_custom_call" | custom-call | tf_op jit(solution)/shard_map/attention_back_and_sum/pallas_call | solution.py:512
  95.0 1.0 slice_bitcast_fusion
  95.9 0.9 copy.29
  96.9 0.8 constant_dynamic-slice_fusion
  97.6 0.5 slice_bitcast_fusion.2
  98.2 2.4 %unpack.1 = (f32[96,1152]{1,0:T(8,128)}, f32[96,384]{1,0:T(8,128)}, f32[96,1536]{1,0:T(8,128)}, f32[384,384]{1,0:T(8,128)}) custom-call(bf16[96,3072]{1,0:T(8,128)(2,1)} %get-tuple-element.48.a_ref, bf16[96,1536]{1,0:T(8,128)(2,1)} %get-tuple-element.49.b_ref), custom_call_target="tpu_custom_call" | custom-call | tf_op jit(solution)/shard_map/unpack/pallas_call | solution.py:554
  100.5 0.7 slice.31
  101.2 0.6 dynamic_slice.10
  101.9 1.3 %dynamic-slice_reduce_fusion = f32[384]{0:T(512)} fusion(f32[16,384]{1,0:T(8,128)} %get-tuple-element.47, s32[]{:T(128)S(6)} %select_n.44), kind=kLoop, calls=%fused_computation.15 | loop fusion | bytes 3076 | tf_op jit(solution)/shard_map/dynamic_slice | solution.py:605
  (7 shorter events, 0.1 us)

commit v3 on v2

--- a/solution.py
+++ b/solution.py
@@ -69,89 +69,54 @@
     return over_z, plane, twin
 
 
-def gather_kernel(
-    wh_ref, wm_ref, we_ref, wr_ref, x_ref, s_ref, w_all, x_all, s_all,
-    zs, zr, xs, xr, ss, sr, ps, pr, cs, cr, loc,
-):
-    rep, z, core, spot, base = places()
-    over_z, plane, twin = team_devices()
-    half = w_all.shape[1] // 2
-    cols = w_all.shape[2] // 4
-    rows = pl.ds(pl.multiple_of(core * half, 16), half)
-    part = pl.ds(pl.multiple_of(spot * cols, 128), cols)
-    depth, width = wm_ref.shape
-    c1, c2, c3 = 3 * width, 4 * width, 8 * width
-    w_all[z, :, :c1] = wh_ref[...]
-    w_all[z, :, c1:c2] = wm_ref[...]
-    w_all[z, :, c2:c3] = we_ref[...]
-    for j in range(4):
-        w_all[z, :, c3 + j * width : c3 + (j + 1) * width] = wr_ref[j * depth : (j + 1) * depth, :]
-    greet(over_z + plane + [twin])
-    copies = []
-    for d in (1, 2, 3):
-        copy = remote(w_all.at[z, rows, part], w_all.at[z, rows, part], zs.at[d], zr.at[d], over_z[d - 1])
+class Fetch:
+    def __init__(self, w, zs, zr, ps, pr, cs, cr):
+        self.__dict__.update(locals())
+        rep, self.z, core, spot, base = places()
+        self.over_z, self.plane, self.twin = team_devices()
+        half, cols = w.shape[1] // 2, w.shape[2] // 4
+        self.rows = pl.ds(pl.multiple_of(core * half, 16), half)
+        self.part = pl.ds(pl.multiple_of(spot * cols, 128), cols)
+        self.sent = []
+
+    def go(self, here, *args):
+        copy = remote(here, here, *args)
         copy.start()
-        copies.append(copy)
-    others = []
-    for d in (1, 2, 3):
-        a = remote(x_ref, x_all.at[z], xs.at[d], xr.at[d], over_z[d - 1])
-        b = remote(s_ref, s_all.at[z], ss.at[d], sr.at[d], over_z[d - 1])
-        a.start()
-        b.start()
-        others += [a, b]
-    locals_ = []
-    for k, (src, dst) in enumerate(((x_ref, x_all), (s_ref, s_all))):
-        copy = pltpu.make_async_copy(src, dst.at[z], loc.at[k])
-        copy.start()
-        locals_.append(copy)
-    spread = {}
-    for d in (1, 2, 3):
-        copies[d - 1].wait_recv()
-        owner = lax.rem(z + 4 - d, 4)
-        for e in (1, 2, 3):
-            here = w_all.at[owner, rows, part]
-            copy = remote(here, here, ps.at[d * 3 + e - 4], pr.at[d * 3 + e - 4], plane[e - 1])
-            copy.start()
-            spread[d, e] = copy
-    crossed = []
-    for d in (1, 2, 3):
-        owner = lax.rem(z + 4 - d, 4)
-        for e in (1, 2, 3):
-            spread[d, e].wait_recv()
-        here = w_all.at[owner, rows]
-        copy = remote(here, here, cs.at[d], cr.at[d], twin)
-        copy.start()
-        crossed.append(copy)
-    for copy in locals_:
-        copy.wait()
-    for copy in others:
-        copy.wait()
-    for copy in copies:
-        copy.wait_send()
-    for copy in spread.values():
-        copy.wait_send()
-    for copy in crossed:
-        copy.wait()
-
-
-def gather_call(weights, x, s):
-    dma = pltpu.SemaphoreType.DMA
-    depth, width = weights[1].shape
-    return pl.pallas_call(
-        gather_kernel,
-        out_shape=[
-            jax.ShapeDtypeStruct((4, depth, 12 * width), bf16),
-            jax.ShapeDtypeStruct((4,) + x.shape, bf16),
-            jax.ShapeDtypeStruct((4,) + s.shape, bf16),
-        ],
-        in_specs=[pl.BlockSpec(memory_space=VMEM)] * 6,
-        out_specs=[pl.BlockSpec(memory_space=VMEM)] * 3,
-        scratch_shapes=[dma((4,))] * 6 + [dma((9,))] * 2 + [dma((4,))] * 2 + [dma((2,))],
-        compiler_params=pltpu.CompilerParams(
-            collective_id=0, has_side_effects=True, vmem_limit_bytes=LIMIT
-        ),
-        name="gather",
-    )(*weights, x, s)
+        self.sent.append(copy)
+        return copy
+
+    def to_group(self):
+        self.first = {}
+        for d in (1, 2, 3):
+            here = self.w.at[self.z, self.rows, self.part]
+            self.first[d] = self.go(here, self.zs.at[d], self.zr.at[d], self.over_z[d - 1])
+
+    def to_plane(self):
+        self.second = {}
+        for d in (1, 2, 3):
+            owner = lax.rem(self.z + 4 - d, 4)
+            self.first[d].wait_recv()
+            for e in (1, 2, 3):
+                here = self.w.at[owner, self.rows, self.part]
+                k = d * 3 + e - 4
+                self.second[d, e] = self.go(here, self.ps.at[k], self.pr.at[k], self.plane[e - 1])
+
+    def to_twin(self):
+        self.third = []
+        for d in (1, 2, 3):
+            owner = lax.rem(self.z + 4 - d, 4)
+            for e in (1, 2, 3):
+                self.second[d, e].wait_recv()
+            here = self.w.at[owner, self.rows]
+            self.third.append(self.go(here, self.cs.at[d], self.cr.at[d], self.twin))
+
+    def arrive(self):
+        for copy in self.third:
+            copy.wait_recv()
+
+    def finish(self):
+        for copy in self.sent:
+            copy.wait_send()
 
 
 class Flow:
@@ -280,24 +245,49 @@
 
 
 def first_kernel(
-    span, valid_ref, w_ref, x_all, s_ref, x_ref, oc_ref,
-    out_ref, ga_ref, g_ref, gm_ref, v_ref, mc_ref, st_ref, qkv_ref, dq_ref,
-    mixed_s, mc_s, prob_s, wr_s,
+    span, valid_ref, wh_in, wm_in, we_in, wr_in, x_ref, s_in, oc_ref,
+    out_ref, ga_ref, g_ref, gm_ref, v_ref, mc_ref, st_ref, qkv_ref, dq_ref, wb_ref, s_ref,
+    mixed_s, mc_s, prob_s, wr_s, x_all, wa_ref, xs, xr, ss, sr, *sems,
 ):
+    fb = Fetch(wb_ref, *sems[:6])
+    fa = Fetch(wa_ref, *sems[6:])
+    over_z, plane, twin = team_devices()
     z = lax.axis_index("grp")
     valid = valid_ref[0]
     n, padded, width = x_all.shape
-    depth = w_ref.shape[1]
+    depth = wb_ref.shape[1]
     hidden = 4 * width
+    c1, c2 = 3 * width, 4 * width
+    wb_ref[z, :, :c1] = wh_in[...]
+    wb_ref[z, :, c1:] = wm_in[...]
+    wa_ref[z, :, :c2] = we_in[...]
+    for j in range(4):
+        wa_ref[z, :, c2 + j * width : c2 + (j + 1) * width] = wr_in[j * depth : (j + 1) * depth, :]
+    greet(over_z + plane + [twin])
+    fb.to_group()
+    others = []
+    for d in (1, 2, 3):
+        p = remote(s_in, s_ref.at[z], ss.at[d], sr.at[d], over_z[d - 1])
+        q = remote(x_ref, x_all.at[z], xs.at[d], xr.at[d], over_z[d - 1])
+        p.start()
+        q.start()
+        others += [p, q]
+    fa.to_group()
+    x_all[z] = x_ref[...]
+    s_ref[z] = s_in[...]
+    fb.to_plane()
+    for copy in others:
+        copy.wait()
+    fa.to_plane()
+    fb.to_twin()
     vec = s_ref[0].astype(f32) + s_ref[1].astype(f32) + s_ref[2].astype(f32) + s_ref[3].astype(f32)
     gain1, bias1, mixb, gain2, bias2, redb = [vec[i : i + 1] for i in range(6)]
     hb_q, hb_v = vec[6:7], vec[7:8]
     expb = jnp.concatenate([vec[8:9], vec[9:10], vec[10:11], vec[11:12]], 1)
-    c1, c2, c3 = 3 * width, 4 * width, 8 * width
-
-    w_heads = w_ref[:, :, :c1].reshape(width, c1)
     unit, _ = normed(x_all[...].reshape(n * padded, width).astype(f32))
     low = (unit * gain1 + bias1).astype(bf16)
+    fb.arrive()
+    w_heads = wb_ref[:, :, :c1].reshape(width, c1)
     proj = dot_nn(low, w_heads)
     qkv_ref[:, :width] = (proj[:, :width] + hb_q).astype(bf16)
     qkv_ref[:, width : 2 * width] = proj[:, width : 2 * width].astype(bf16)
@@ -319,12 +309,14 @@
         prob_s[head] = prob
         lses.append(top + jnp.log(row))
         mixed_s[:, lo : lo + HEAD_DIM] = dot_nn(prob.astype(bf16), v).astype(bf16)
-    w_mix = w_ref[:, :, c1:c2].reshape(width, width)
+    fa.to_twin()
+    w_mix = wb_ref[:, :, c1:].reshape(width, width)
     mixed = mixed_s[...]
     after = x_ref[...].astype(f32) + dot_nn(mixed, w_mix) + mixb
     unit2, inv2 = normed(after)
     low2 = (unit2 * gain2 + bias2).astype(bf16)
-    w_exp = w_ref[:, :, c2:c3].reshape(width, hidden)
+    fa.arrive()
+    w_exp = wa_ref[:, :, :c2].reshape(width, hidden)
     pre = dot_nn(low2, w_exp) + expb
     cube = 0.044715
     root = 0.7978845608028654
@@ -334,7 +326,7 @@
     for i in range(n):
         for j in range(4):
             lo = i * width + j * depth
-            wr_s[lo : lo + depth, :] = w_ref[i, :, c3 + j * width : c3 + (j + 1) * width]
+            wr_s[lo : lo + depth, :] = wa_ref[i, :, c2 + j * width : c2 + (j + 1) * width]
     w_red = wr_s[...]
     out_ref[...] = (after + dot_nn(act, w_red) + redb).astype(bf16)
 
@@ -379,10 +371,16 @@
         stats = jnp.where(lane == head, lses[head], stats)
         stats = jnp.where(lane == head + 8, cols[head], stats)
     st_ref[...] = stats.T[:ROWS, :]
-
-
-def first_call(span, valid, w, x_all, s, x, oc):
-    n, padded, width = x_all.shape
+    fb.finish()
+    fa.finish()
+
+
+def first_call(span, valid, weights, x, s, oc):
+    n = 4
+    padded, width = x.shape
+    depth = weights[1].shape[0]
+    dma = pltpu.SemaphoreType.DMA
+    fetch = [dma((4,)), dma((4,)), dma((9,)), dma((9,)), dma((4,)), dma((4,))]
     shape = jax.ShapeDtypeStruct
     vmem = pl.BlockSpec(memory_space=VMEM)
     return pl.pallas_call(
@@ -390,25 +388,32 @@
         out_shape=[
             shape((padded, width), bf16),
             shape((padded, width), f32),
-            shape((n, w.shape[1], 8 * width), bf16),
-            shape((n, w.shape[1], width), bf16),
+            shape((n, depth, 8 * width), bf16),
+            shape((n, depth, width), bf16),
             shape((ROWS, width), f32),
             shape((padded, width), bf16),
             shape((ROWS, padded), f32),
             shape((n * padded, 3 * width), bf16),
             shape((padded, width), bf16),
+            shape((n, depth, 4 * width), bf16),
+            shape((n,) + s.shape, bf16),
         ],
-        in_specs=[pl.BlockSpec(memory_space=pltpu.SMEM)] + [vmem] * 5,
-        out_specs=[vmem] * 9,
+        in_specs=[pl.BlockSpec(memory_space=pltpu.SMEM)] + [vmem] * 7,
+        out_specs=[vmem] * 11,
         scratch_shapes=[
             VMEM((padded, width), bf16),
             VMEM((padded, width), bf16),
             VMEM((HEADS, padded, n * padded), f32),
             VMEM((4 * width, width), bf16),
-        ],
-        compiler_params=pltpu.CompilerParams(vmem_limit_bytes=LIMIT),
-        name="forward_and_feed_back",
-    )(valid, w, x_all, s, x, oc)
+            VMEM((n, padded, width), bf16),
+            VMEM((n, depth, 8 * width), bf16),
+            dma((4,)), dma((4,)), dma((4,)), dma((4,)),
+        ] + fetch + fetch,
+        compiler_params=pltpu.CompilerParams(
+            collective_id=0, has_side_effects=True, vmem_limit_bytes=LIMIT
+        ),
+        name="gather_forward_and_feed_back",
+    )(valid, *weights, x, s, oc)
 
 
 def second_kernel(
@@ -589,8 +594,9 @@
     ).astype(bf16)
 
     weights = (heads_weight, mixing_weight, expand_weight, reduce_weight)
-    w_all, x_all, s_all = gather_call(weights, x, s)
-    out, ga, g, gm, v, mc, st, qkv, dq = first_call(span, valid_count, w_all, x_all, s_all, x, oc)
+    out, ga, g, gm, v, mc, st, qkv, dq, w_all, s_all = first_call(
+        span, valid_count, weights, x, s, oc
+    )
     ig, ga_sum, gb_sum, v = second_call(
         span, valid_count, w_all, s_all, x, ga, mc, st, qkv, dq, g, gm, v
     )

time: 104 us -> 105 us (level)
    pallas_call x1 -> x0, Pallas kernels: 32 us -> none  [gather_call(): pl.pallas_call(gather_kernel, out_shape=[jax.ShapeDtypeStruct((4, depth,...]
    pallas_call x1, Pallas kernels: 12.9 us -> 44.4 us  [first_call(): pl.pallas_call(functools.partial(first_kernel, span), out_shape=[shape((p...]
    pallas_call x1, Pallas kernels: 41 us -> 42.6 us  [second_call(): pl.pallas_call(functools.partial(second_kernel, span), out_shape=[shape((...]
where the time goes in v3:
time: 105 us; the launch traced here: 104 us
  Pallas kernels  89.3 us (85%)
  local copies, waits for them, and re-layouts  12.1 us (12%)
  other arithmetic  1.42 us (1%)
  between operations  1.34 us (1%)
    pallas_call x1, Pallas kernels, first_call(): pl.pallas_call(functools.partial(first_kernel, span), out_shape=[shape((p...  44.4 us
    pallas_call x1, Pallas kernels, second_call(): pl.pallas_call(functools.partial(second_kernel, span), out_shape=[shape((...  42.6 us
    pad x2, local copies, waits for them, and re-layouts, pad_rows(): return jnp.pad(x[0], ((0, padded - span), (0, 0)))  3.13 us
    pallas_call x1, Pallas kernels, unpack_call(): pl.pallas_call(unpack_kernel, out_shape=[shape((depth, 3 * width), f32),...  2.35 us

profile of v3, /device:TPU:0, one launch (start us, length us, event | category | flops | bytes accessed | tf_op | source)
XLA Modules:
  0.0 104.2 jit_solution(7377720985342738744)
XLA Ops:
  1.3 1.6 %pad.7.x_ref = bf16[160,384]{1,0:T(8,128)(2,1)} pad(bf16[145,384]{1,0:T(8,128)(2,1)} %bitcast.24, bf16[]{:T(256)} %constant.30.clone.1), padding=0_15x0_0 | pad | bytes 234242 | tf_op jit(solution)/shard_map/jit(_pad)/pad | solution.py:583
  2.9 0.8 broadcast_select_fusion.1
  3.6 0.7 tile.22
  4.3 0.1 tile.23
  4.4 0.8 stack.27
  5.2 0.1 tile.21
  5.3 0.6 pad_maximum_fusion.s_in
  5.9 1.6 %pad.8.oc_ref = bf16[160,384]{1,0:T(8,128)(2,1)} pad(bf16[145,384]{1,0:T(8,128)(2,1)} %bitcast.25, bf16[]{:T(256)} %constant.30.clone.1), padding=0_15x0_0 | pad | bytes 234242 | tf_op jit(solution)/shard_map/jit(_pad)/pad | solution.py:583
  7.5 44.4 %gather_forward_and_feed_back.1 = (bf16[160,384]{1,0:T(8,128)(2,1)}, f32[160,384]{1,0:T(8,128)}, bf16[4,96,3072]{2,1,0:T(8,128)(2,1)}, bf16[4,96,384]{2,1,0:T(8,...) custom-call(s32[1]{0:T(128)S(6)} %copy.30.valid_ref, ...), custom_call_target="tpu_custom_call" | custom-call | tf_op jit(solution)/shard_map/gather_forward_and_feed_back/pallas_call | solution.py:386
  51.8 1.6 %slice_bitcast_fusion.1 = bf16[1,145,384]{2,1,0:T(8,128)(2,1)} fusion(bf16[160,384]{1,0:T(8,128)(2,1)} %get-tuple-element.33), kind=kLoop, calls=%fused_computation.1 | loop fusion | bytes 222720 | tf_op jit(solution)/shard_map/broadcast_in_dim | solution.py:613
  53.4 42.6 %attention_back_and_sum.1 = (f32[160,384]{1,0:T(8,128)}, bf16[96,3072]{1,0:T(8,128)(2,1)}, bf16[96,1536]{1,0:T(8,128)(2,1)}, f32[16,384]{1,0:T(8,128)}) custom-call(s32[1]{0:T(128)S(6)} %copy.30.valid_ref, bf16[4,96,1536]{2,1,0:T(8,128)(2,1)} %get-tuple-element.34.w_ref, bf16[4,16,384]{2,1,0:T(8,128)(2,1)} %get-tuple-element.35.s_ref, ...), custom_call_target="tpu_custom_call" | custom-call | tf_op jit(solution)/shard_map/attention_back_and_sum/pallas_call | solution.py:517
  96.0 1.0 slice_bitcast_fusion
  96.9 0.9 copy.29
  97.9 0.8 constant_dynamic-slice_fusion
  98.6 0.5 slice_bitcast_fusion.2
  99.2 2.4 %unpack.1 = (f32[96,1152]{1,0:T(8,128)}, f32[96,384]{1,0:T(8,128)}, f32[96,1536]{1,0:T(8,128)}, f32[384,384]{1,0:T(8,128)}) custom-call(bf16[96,3072]{1,0:T(8,128)(2,1)} %get-tuple-element.46.a_ref, bf16[96,1536]{1,0:T(8,128)(2,1)} %get-tuple-element.47.b_ref), custom_call_target="tpu_custom_call" | custom-call | tf_op jit(solution)/shard_map/unpack/pallas_call | solution.py:559
  101.5 0.7 slice.31
  102.2 0.6 dynamic_slice.10
  102.9 1.3 %dynamic-slice_reduce_fusion = f32[384]{0:T(512)} fusion(f32[16,384]{1,0:T(8,128)} %get-tuple-element.45, s32[]{:T(128)S(6)} %select_n.44), kind=kLoop, calls=%fused_computation.15 | loop fusion | bytes 3076 | tf_op jit(solution)/shard_map/dynamic_slice | solution.py:611
  (7 shorter events, 0.1 us)

commit v4 on v3

--- a/solution.py
+++ b/solution.py
@@ -265,6 +265,7 @@
         wa_ref[z, :, c2 + j * width : c2 + (j + 1) * width] = wr_in[j * depth : (j + 1) * depth, :]
     greet(over_z + plane + [twin])
     fb.to_group()
+    fa.to_group()
     others = []
     for d in (1, 2, 3):
         p = remote(s_in, s_ref.at[z], ss.at[d], sr.at[d], over_z[d - 1])
@@ -272,14 +273,13 @@
         p.start()
         q.start()
         others += [p, q]
-    fa.to_group()
     x_all[z] = x_ref[...]
     s_ref[z] = s_in[...]
     fb.to_plane()
+    fa.to_plane()
+    fb.to_twin()
     for copy in others:
         copy.wait()
-    fa.to_plane()
-    fb.to_twin()
     vec = s_ref[0].astype(f32) + s_ref[1].astype(f32) + s_ref[2].astype(f32) + s_ref[3].astype(f32)
     gain1, bias1, mixb, gain2, bias2, redb = [vec[i : i + 1] for i in range(6)]
     hb_q, hb_v = vec[6:7], vec[7:8]

time: 105 us -> 101 us (0.962)
  Pallas kernels: 89.3 us -> 85.2 us
    pallas_call x1, Pallas kernels: 44.4 us -> 40.4 us  [first_call(): pl.pallas_call(functools.partial(first_kernel, span), out_shape=[shape((p...]
where the time goes in v4:
time: 101 us; the launch traced here: 100 us
  Pallas kernels  85.2 us (84%)
  local copies, waits for them, and re-layouts  12.1 us (12%)
  other arithmetic  1.42 us (1%)
  between operations  1.34 us (1%)
    pallas_call x1, Pallas kernels, second_call(): pl.pallas_call(functools.partial(second_kernel, span), out_shape=[shape((...  42.4 us
    pallas_call x1, Pallas kernels, first_call(): pl.pallas_call(functools.partial(first_kernel, span), out_shape=[shape((p...  40.4 us
    pad x2, local copies, waits for them, and re-layouts, pad_rows(): return jnp.pad(x[0], ((0, padded - span), (0, 0)))  3.13 us
    pallas_call x1, Pallas kernels, unpack_call(): pl.pallas_call(unpack_kernel, out_shape=[shape((depth, 3 * width), f32),...  2.35 us

profile of v4, /device:TPU:0, one launch (start us, length us, event | category | flops | bytes accessed | tf_op | source)
XLA Modules:
  0.0 100.1 jit_solution(12107650243091462447)
XLA Ops:
  1.3 1.6 %pad.7.x_ref = bf16[160,384]{1,0:T(8,128)(2,1)} pad(bf16[145,384]{1,0:T(8,128)(2,1)} %bitcast.24, bf16[]{:T(256)} %constant.30.clone.1), padding=0_15x0_0 | pad | bytes 234242 | tf_op jit(solution)/shard_map/jit(_pad)/pad | solution.py:583
  2.9 0.8 broadcast_select_fusion.1
  3.6 0.7 tile.22
  4.3 0.1 tile.23
  4.4 0.8 stack.27
  5.2 0.1 tile.21
  5.3 0.6 pad_maximum_fusion.s_in
  5.9 1.6 %pad.8.oc_ref = bf16[160,384]{1,0:T(8,128)(2,1)} pad(bf16[145,384]{1,0:T(8,128)(2,1)} %bitcast.25, bf16[]{:T(256)} %constant.30.clone.1), padding=0_15x0_0 | pad | bytes 234242 | tf_op jit(solution)/shard_map/jit(_pad)/pad | solution.py:583
  7.5 40.4 %gather_forward_and_feed_back.1 = (bf16[160,384]{1,0:T(8,128)(2,1)}, f32[160,384]{1,0:T(8,128)}, bf16[4,96,3072]{2,1,0:T(8,128)(2,1)}, bf16[4,96,384]{2,1,0:T(8,...) custom-call(s32[1]{0:T(128)S(6)} %copy.30.valid_ref, ...), custom_call_target="tpu_custom_call" | custom-call | tf_op jit(solution)/shard_map/gather_forward_and_feed_back/pallas_call | solution.py:386
  47.9 1.6 %slice_bitcast_fusion.1 = bf16[1,145,384]{2,1,0:T(8,128)(2,1)} fusion(bf16[160,384]{1,0:T(8,128)(2,1)} %get-tuple-element.33), kind=kLoop, calls=%fused_computation.1 | loop fusion | bytes 222720 | tf_op jit(solution)/shard_map/broadcast_in_dim | solution.py:613
  49.4 42.4 %attention_back_and_sum.1 = (f32[160,384]{1,0:T(8,128)}, bf16[96,3072]{1,0:T(8,128)(2,1)}, bf16[96,1536]{1,0:T(8,128)(2,1)}, f32[16,384]{1,0:T(8,128)}) custom-call(s32[1]{0:T(128)S(6)} %copy.30.valid_ref, bf16[4,96,1536]{2,1,0:T(8,128)(2,1)} %get-tuple-element.34.w_ref, bf16[4,16,384]{2,1,0:T(8,128)(2,1)} %get-tuple-element.35.s_ref, ...), custom_call_target="tpu_custom_call" | custom-call | tf_op jit(solution)/shard_map/attention_back_and_sum/pallas_call | solution.py:517
  91.9 1.0 slice_bitcast_fusion
  92.8 0.9 copy.29
  93.7 0.8 constant_dynamic-slice_fusion
  94.5 0.5 slice_bitcast_fusion.2
  95.0 2.4 %unpack.1 = (f32[96,1152]{1,0:T(8,128)}, f32[96,384]{1,0:T(8,128)}, f32[96,1536]{1,0:T(8,128)}, f32[384,384]{1,0:T(8,128)}) custom-call(bf16[96,3072]{1,0:T(8,128)(2,1)} %get-tuple-element.46.a_ref, bf16[96,1536]{1,0:T(8,128)(2,1)} %get-tuple-element.47.b_ref), custom_call_target="tpu_custom_call" | custom-call | tf_op jit(solution)/shard_map/unpack/pallas_call | solution.py:559
  97.4 0.7 slice.31
  98.1 0.6 dynamic_slice.10
  98.8 1.3 %dynamic-slice_reduce_fusion = f32[384]{0:T(512)} fusion(f32[16,384]{1,0:T(8,128)} %get-tuple-element.45, s32[]{:T(128)S(6)} %select_n.44), kind=kLoop, calls=%fused_computation.15 | loop fusion | bytes 3076 | tf_op jit(solution)/shard_map/dynamic_slice | solution.py:611
  (7 shorter events, 0.1 us)
